TPU v7x, 256 devices: a whole 4x4x8 slice. The times are simulated.
256 devices in a mesh: expert: 16 (over x_hi, y, core), cuts: 16 (over z, x_lo).
Axes of the slice: x: 4 (x_hi: 2, x_lo: 2; x = x_hi * 2 + x_lo), y: 4, z: 8, core: 2. Of those that a mesh axis runs over, the one named last changes fastest.
Arguments:
- tokens: bfloat16 [2048, 6144], P('expert'), may hold values from -6 to 6
- routes: int32 [2048, 4], P('expert'), may hold values from 0 to 15, all different within a row; in each aligned block of 128 rows (0 to 127, 128 to 255, ...) at most 64 rows name the same one
- route_weights: float32 [2048, 4], P('expert'), may hold values from 0.1 to 1
- w_gate: bfloat16 [16, 5376, 6144], P('expert', 'cuts'), may hold values from -0.078125 to 0.078125
- w_down: bfloat16 [16, 5376, 6144], P('expert', 'cuts'), may hold values from -0.078125 to 0.078125
Outputs:
- mixed: bfloat16 [2048, 6144], P('expert')
Inputs may be any that keep to these rules, and one draw needn't show every extreme that they name: `routes`: each row names 4 different experts. In each aligned block of 128 rows (the rows of one index of expert) no expert is named by more than 64 rows, a bound that some block reaches.
All inputs are finite; a program needn't handle non-finite values.
Results may differ from a plain program's by a relative error of at most 0.025.
Values may be sent and summed in bfloat16 or wider, within the bound.
A program may use at most 64 MiB of HBM per device.

v0:
```python
import jax
import jax.numpy as jnp
from jax import lax
from jax.sharding import PartitionSpec as P


def on_device(tokens, routes, route_weights, w_gate, w_down):
    tok_count, feature_count = tokens.shape
    top_count = routes.shape[1]
    n_groups = lax.axis_size("expert")
    n_slices = lax.axis_size("cuts")
    capacity = min(tok_count, 2 * tok_count * top_count // n_groups)
    share = capacity // n_slices
    slice_index = lax.axis_index("cuts")
    gate_rows = w_gate[0]
    down_rows = w_down[0]
    one_hot = (routes[:, :, None] == jnp.arange(n_groups, dtype=jnp.int32)[None, None, :]).astype(
        jnp.int32
    )
    flat_hits = one_hot.reshape(tok_count * top_count, n_groups)
    earlier = jnp.cumsum(flat_hits, 0) - flat_hits
    slot_index = jnp.sum(earlier * flat_hits, 1).reshape(tok_count, top_count)
    target = routes * capacity + slot_index
    places = (
        jnp.arange(n_groups, dtype=jnp.int32)[:, None] * capacity
        + slice_index * share
        + jnp.arange(share, dtype=jnp.int32)[None, :]
    ).reshape(-1)
    matches = target[None, :, :] == places[:, None, None]
    selector = jnp.any(matches, 2).astype(jnp.bfloat16)
    outgoing = jnp.dot(selector, tokens, preferred_element_type=jnp.float32).astype(jnp.bfloat16)
    outgoing = outgoing.reshape(n_groups, share, feature_count)
    arrived = lax.all_to_all(outgoing, "expert", split_axis=0, concat_axis=0, tiled=True)
    piece = lax.all_gather(arrived, "cuts", axis=1, tiled=True)
    flat_rows = piece.reshape(-1, feature_count)
    pre_act = lax.dot_general(
        flat_rows, gate_rows, (((1,), (1,)), ((), ())), preferred_element_type=jnp.float32
    )
    hidden = (
        jax.nn.silu(pre_act)
        .astype(jnp.bfloat16)
        .reshape(piece.shape[0], piece.shape[1], gate_rows.shape[0])
    )
    cut_terms = jnp.einsum("rcf,fd->rcd", hidden, down_rows, preferred_element_type=jnp.float32)
    summed = lax.psum_scatter(
        cut_terms.astype(jnp.bfloat16), "cuts", scatter_dimension=1, tiled=True
    )
    returned = lax.all_to_all(summed, "expert", split_axis=0, concat_axis=0, tiled=True)
    weighting = jnp.sum(
        jnp.where(matches, route_weights[None, :, :], jnp.zeros_like(route_weights)[None, :, :]), 2
    )
    slot_part = jnp.dot(
        weighting.T,
        returned.reshape(-1, feature_count).astype(jnp.float32),
        precision=lax.Precision.HIGHEST,
    )
    mixed = lax.psum(slot_part.astype(jnp.bfloat16), "cuts")
    return mixed


def solution(mesh):
    in_specs = (
        P("expert", None),
        P("expert", None),
        P("expert", None),
        P("expert", "cuts", None),
        P("expert", "cuts", None),
    )
    out_specs = P("expert", None)
    return jax.shard_map(
        on_device, mesh=mesh, in_specs=in_specs, out_specs=out_specs, check_vma=False
    )
```

profile of v0, /device:TPU:2, one launch (start us, length us, event | category | flops | bytes accessed | tf_op | source)
XLA Modules:
  0.0 798.1 jit_solution(9430609528039624192)
XLA Ops:
  6.5 0.0 copy-start
  6.5 0.0 all-gather.2.cloned.1.call-start
  6.5 0.9 copy.58
  7.4 0.1 eq.43
  7.6 0.1 eq.39
  7.7 1.2 reduce-window.6
  8.8 0.2 slice_reduce_fusion
  9.1 0.1 fusion.8
  9.2 0.1 reshape.57
  9.3 0.1 copy.61
  9.4 0.7 multiply_add_fusion
  10.1 0.1 iota_add_fusion
  10.2 0.1 add.48
  10.2 0.1 compare_reduce_fusion
  10.3 0.0 copy-done
  10.4 0.4 convolution_convert_fusion.2
  10.7 0.3 reshape.58
  11.0 21.1 %all_to_all.10 = bf16[16,4,6144]{2,1,0:T(4,128)(2,1)S(1)} all-to-all(bf16[16,4,6144]{2,1,0:T(4,128)(2,1)S(1)} %reshape.58), channel_id=1, replica_groups=mesh['expert'=16,'cuts'=16] {'expert'}, dimensions={0} | all-to-all | bytes 1572864 | tf_op jit(solution)/shard_map/all_to_all | solution.py:33
  32.1 1.3 copy.62
  33.4 0.0 all-gather.2.cloned.1.call-update
  33.5 0.0 reduce-scatter.2.cloned.1.call-start
  33.5 265.3 %all-gather.2.cloned.1.call-done = bf16[16,64,6144]{2,0,1:T(8,128)(2,1)} async-done(((bf16[16,4,6144]{2,0,1:T(8,128)(2,1)}), bf16[16,64,6144]{2,0,1:T(8,128)(2,1)}) %all-gather.2.cloned.1.call-update) | async-done | bytes 12582928 | tf_op jit(solution)/shard_map/all_gather | solution.py:34
  298.8 0.0 copy-start.3
  298.8 11.9 %copy.63 = bf16[16,64,6144]{2,1,0:T(8,128)(2,1)S(1)} copy(bf16[16,64,6144]{2,0,1:T(8,128)(2,1)} %all-gather.2.cloned.1.call-done) | data formatting | bytes 25165824 | tf_op jit(solution)/shard_map/all_gather | solution.py:34
  310.7 0.0 copy-done.3
  310.7 4.6 multiply_convert_fusion
  315.4 0.4 copy.64
  315.7 9.1 %convolution_convert_fusion = bf16[16,64,6144]{2,1,0:T(8,128)(2,1)S(1)} fusion(bf16[16,64,336]{2,1,0:T(8,128)(2,1)S(1)} %bitcast.37, bf16[1,336,6144]{2,1,0:T(8,128)(2,1)} %param.9), kind=kOutput, calls=%fused_computation | convolution fusion | flops 4234149888 | bytes 17399808 | tf_op jit(solution)/shard_map/rcf,fd->rcd/dot_general | solution.py:44
  324.9 26.9 %copy.65 = bf16[16,64,6144]{2,0,1:T(8,128)(2,1)} copy(bf16[16,64,6144]{2,1,0:T(8,128)(2,1)S(1)} %convolution_convert_fusion) | data formatting | bytes 25165824 | tf_op jit(solution)/shard_map/convert_element_type | solution.py:46
  351.7 0.0 copy-start.2
  351.7 0.0 reduce-scatter.2.cloned.1.call-update
  351.7 269.7 %reduce-scatter.2.cloned.1.call-done = bf16[16,4,6144]{2,0,1:T(8,128)(2,1)} async-done(((bf16[16,64,6144]{2,0,1:T(8,128)(2,1)}), bf16[16,4,6144]{2,0,1:T(8,128)(2,1)}) %reduce-scatter.2.cloned.1.call-update) | async-done | bytes 786448 | tf_op jit(solution)/shard_map/reduce_scatter | solution.py:45
  621.4 2.6 copy.66
  624.0 6.4 all-to-all-start.1
  630.5 0.0 all-reduce.2.cloned.1.call-start
  630.5 0.0 copy-done.2
  630.6 0.0 copy-start.1
  630.6 0.1 fusion.5
  630.7 15.1 %all-to-all-done.1 = bf16[16,4,6144]{2,1,0:T(4,128)(2,1)S(1)} async-done(((bf16[16,4,6144]{2,1,0:T(4,128)(2,1)}), bf16[16,4,6144]{2,1,0:T(4,128)(2,1)S(1)}, u32[]{:S(2)}, u32[]{:S(2)}) %all-to-all-start.1) | async-done | bytes 786464 | tf_op jit(solution)/shard_map/all_to_all | solution.py:48
  645.7 0.2 reshape.61
  645.9 2.6 convolution_convert_fusion.1
  648.5 0.0 all-reduce.2.cloned.1.call-update
  648.5 140.4 %all-reduce.2.cloned.1.call-done = bf16[128,6144]{1,0:T(8,128)(2,1)} async-done(((bf16[128,6144]{1,0:T(8,128)(2,1)}), bf16[128,6144]{1,0:T(8,128)(2,1)}) %all-reduce.2.cloned.1.call-update) | async-done | bytes 1572880 | tf_op jit(solution)/shard_map/psum | solution.py:57
  788.9 2.7 copy.70
  791.6 0.0 copy-done.1
  (4 shorter events, 0.1 us)
Async XLA Ops:
  6.5 3.8 copy-start
  6.5 292.3 %all-gather.2.cloned.1.call-start = ((), (), s32[]{:S(2)}) async-start(), calls=%async_computation.3 | async-start | bytes 13369344 | tf_op jit(solution)/shard_map/all_gather | solution.py:34
  33.5 588.0 %reduce-scatter.2.cloned.1.call-start = ((), (), s32[]{:S(2)}) async-start(), calls=%async_computation.4 | async-start | bytes 13369344 | tf_op jit(solution)/shard_map/reduce_scatter | solution.py:45
  298.8 11.9 %copy-start.3 = (bf16[1,336,6144]{2,1,0:T(8,128)(2,1)S(1)}, bf16[1,336,6144]{2,1,0:T(8,128)(2,1)}, u32[]{:S(2)}) copy-start(bf16[1,336,6144]{2,1,0:T(8,128)(2,1)} %param.8) | copy-start | bytes 12386308
  351.7 278.8 %copy-start.2 = (f32[128,4]{0,1:T(4,128)S(1)}, f32[128,4]{0,1:T(4,128)}, u32[]{:S(2)}) copy-start(f32[128,4]{0,1:T(4,128)} %param.7) | copy-start | bytes 6148
  624.0 21.7 %all-to-all-start.1 = ((bf16[16,4,6144]{2,1,0:T(4,128)(2,1)}), bf16[16,4,6144]{2,1,0:T(4,128)(2,1)S(1)}, u32[]{:S(2)}, u32[]{:S(2)}) async-start(bf16[16,4,6144]{2,1,0:T(4,128)(2,1)} %copy.66), calls=%async_computation.2 | async-start | bytes 1572864 | tf_op jit(solution)/shard_map/all_to_all | solution.py:48
  630.5 158.4 %all-reduce.2.cloned.1.call-start = ((), (), s32[]{:S(2)}) async-start(), calls=%async_computation.5 | async-start | bytes 3145728 | tf_op jit(solution)/shard_map/psum | solution.py:57
  630.6 161.1 %copy-start.1 = (bf16[128,6144]{1,0:T(8,128)(2,1)S(1)}, bf16[128,6144]{1,0:T(8,128)(2,1)}, u32[]{:S(2)}) copy-start(bf16[128,6144]{1,0:T(8,128)(2,1)} %param.5) | copy-start | bytes 4718596
Sparse Core Ops, SparseCore 0:
  33.6 265.2 all-gather.1
  351.9 269.5 reduce-scatter.1
  648.6 140.2 all-reduce.1
where the time goes:
time: 799 us; the launch traced here: 798 us
  waiting for transfers between devices  691 us (86%)
  local copies, waits for them, and re-layouts  47.8 us (6%)
  blocking collectives  21.1 us (3%)
  matrix products  16.7 us (2%)
  between operations  13.2 us (2%)
    reduce_scatter x1, waiting for transfers between devices, on_device(): lax.psum_scatter(cut_terms.astype(jnp.bfloat16), 'cuts', scatter_dimensio...  270 us
    all_gather x1, waiting for transfers between devices, on_device(): piece = lax.all_gather(arrived, 'cuts', axis=1, tiled=True)  265 us
    psum x1, waiting for transfers between devices, on_device(): mixed = lax.psum(slot_part.astype(jnp.bfloat16), 'cuts')  140 us
    convert_element_type x1, local copies, waits for them, and re-layouts, on_device(): cut_terms.astype(jnp.bfloat16)  26.9 us
    all_to_all x1, blocking collectives, on_device(): lax.all_to_all(outgoing, 'expert', split_axis=0, concat_axis=0, tiled=True)  21.1 us
  transfers between devices with their start and end apart: 4, of which 4 were waited for; matrix products, arithmetic and copies ran while one was open for 0% of the time, Pallas kernels for 0%

commit v1 on v0

v1 whole, which is shorter than its diff:
```python
import functools
import jax
import jax.numpy as jnp
from jax import lax
from jax.experimental import pallas as pl
from jax.experimental.pallas import tpu as pltpu
from jax.sharding import PartitionSpec as P

MESH = pl.DeviceIdType.MESH
BF = jnp.bfloat16
F32 = jnp.float32

D = 6144
FF = 336
FF2 = 2 * FF
ROWS = 128
EXPERTS = 16
NS = 12
CW = D // NS
HW = CW // 2
ZP = 4
NI = 2 * NS // 2 - ZP
NP = NS // 2


def kernel(
    wt_ref, tok_ref, wg_ref, wd_ref, o_ref,
    xp, wg, wd, pre, hid, wt,
    ry1, ry2, rx1, rx2, qx1, qx2, qy1, qy2, tz, fz,
    tok_sem, wgo, wgs, wgr, wdo, wds, wdr, wts, wtr,
    s1s, s1r, s2s, s2r, s3s, s3r, s4s, s4r, s5s, s5r,
    y1s, y1r, y2s, y2r, x1s, x1r, x2s, x2r,
    u1s, u1r, u2s, u2r, v1s, v1r, v2s, v2r,
    z1s, z1r, ags, agr, aglo,
):
    e = lax.axis_index("expert")
    c = lax.axis_index("cuts")
    hi, y, k = e // 8, (e // 2) % 4, e % 2
    z, lo = c // 2, c % 2
    ol = 1 - lo

    def dev(hi_, y_, k_, z_, lo_):
        return (hi_ * 8 + y_ * 2 + k_, z_ * 2 + lo_)

    yp = dev(hi, (y + 1) % 4, k, z, lo)
    ym = dev(hi, (y + 3) % 4, k, z, lo)
    inner = dev(hi, y, k, z, ol)
    outer = dev(1 - hi, y, k, z, ol)
    core = dev(hi, y, 1 - k, z, lo)

    def zdev(dz, lo_):
        return dev(hi, y, k, (z + dz) % 8, lo_)

    def rel(dx, dy):
        if dx == 0:
            return dev(hi, (y + dy) % 4, k, z, lo)
        return dev(1 - hi, (y + dy) % 4, k, z, ol)

    def remote(src, dst, ss, rs, to):
        return pltpu.make_async_remote_copy(
            src_ref=src, dst_ref=dst, send_sem=ss, recv_sem=rs, device_id=to, device_id_type=MESH
        )

    def load_tok(s, h):
        return pltpu.make_async_copy(
            tok_ref.at[:, pl.ds(pl.multiple_of(s * CW + h * HW, HW), HW)],
            xp.at[s, h, 0, 0], tok_sem.at[s, h],
        )

    def cols(s):
        return pl.ds(pl.multiple_of(s * CW, CW), CW)

    def load_w(src, dst, sem, s):
        return pltpu.make_async_copy(src.at[0, :, cols(s)], dst.at[s, pl.ds(0, FF)], sem.at[s])

    def swap_w(src, dst, ss, rs, s):
        return remote(src.at[0, :, cols(s)], dst.at[s, pl.ds(FF, FF)], ss.at[s], rs.at[s], core)

    def start_local(s, _):
        load_tok(s, 0).start()
        load_tok(s, 1).start()
        load_w(wg_ref, wg, wgo, s).start()
        load_w(wd_ref, wd, wdo, s).start()
        return 0

    lax.fori_loop(0, NS, start_local, 0)
    wt[0] = wt_ref[...]

    bar = pltpu.get_barrier_semaphore()
    partners = [core]
    for dx in range(2):
        for dy in range(4):
            if (dx, dy) != (0, 0):
                partners.append(rel(dx, dy))
    for dz in range(8):
        if dz:
            partners.append(zdev(dz, lo))
        partners.append(zdev(dz, ol))
    for p in partners:
        pl.semaphore_signal(bar, inc=1, device_id=p, device_id_type=MESH)
    pre[...] = jnp.zeros_like(pre)
    pl.semaphore_wait(bar, len(partners))

    zpar = z % 2

    def item(j):
        return jnp.where(j < ZP, 2 * j + zpar, j + ZP)

    def other(j):
        return 2 * j + 1 - zpar

    def d1(j, d):
        s = item(j)
        return remote(
            xp.at[s, :, 0, 0], xp.at[s, :, 0, 3 if d == 0 else 1],
            s1s.at[j, d], s1r.at[j, d], yp if d == 0 else ym,
        )

    def d2(j, d):
        s = item(j)
        return remote(
            xp.at[s, d, 0, 3 if d == 0 else 1], xp.at[s, d, 0, 2],
            s2s.at[j, d], s2r.at[j, d], yp if d == 0 else ym,
        )

    def d3(j):
        s = item(j)
        return remote(xp.at[s, lo, 0], xp.at[s, lo, 1], s3s.at[j], s3r.at[j], outer)

    def d4(j):
        s = item(j)
        return remote(xp.at[s, ol, 1], xp.at[s, ol, 1], s4s.at[j], s4r.at[j], inner)

    def d5(j, d):
        s = item(j)
        step = jnp.where(j % 2 == 0, 1 - 2 * zpar, 2 * zpar - 1)
        to = dev(hi, y, k, (z + step + 8) % 8, lo)
        if d == 0:
            return remote(xp.at[s, :, 1], xp.at[s, :, 1], s5s.at[j, d], s5r.at[j, d], to)
        mid = xp.at[s, :, 0, pl.ds(1, 3)]
        return remote(mid, mid, s5s.at[j, d], s5r.at[j, d], to)

    def gate(s):
        load_w(wg_ref, wg, wgo, s).wait()
        swap_w(wg_ref, wg, wgs, wgr, s).wait_recv()

        @pl.loop(0, 4)
        def _(i):
            rows = pl.ds(pl.multiple_of(i * 256, 256), 256)
            acc = pre[rows, :]
            for h in range(2):
                xs = xp[s, h, i // 2, pl.ds((i % 2) * 2, 2)].reshape(256, HW)
                ws = wg[s, :, h * HW:(h + 1) * HW]
                acc = acc + lax.dot_general(
                    xs, ws, (((1,), (1,)), ((), ())), preferred_element_type=F32
                )
            pre[rows, :] = acc

    def send_wt():
        for dx in range(2):
            for dy in range(4):
                if (dx, dy) != (0, 0):
                    remote(wt_ref, wt.at[dx * 4 + (4 - dy) % 4], wts, wtr, rel(dx, dy)).start()

    def wait_wt():
        both = wt.at[pl.ds(1, 7)]
        cp = remote(both, both, wts, wtr, core)
        cp.wait_send()
        cp.wait_recv()

    def g_tick(t, _):
        @pl.when(t < NI)
        def _():
            s = item(t)
            load_tok(s, 0).wait()
            load_tok(s, 1).wait()
            d1(t, 0).start()
            d1(t, 1).start()

        @pl.when(t == 0)
        def _():
            send_wt()

        @pl.when(t < NP)
        def _():
            swap_w(wg_ref, wg, wgs, wgr, 2 * t).start()
            swap_w(wg_ref, wg, wgs, wgr, 2 * t + 1).start()

        @pl.when(t >= NP)
        def _():
            @pl.when(t < 2 * NP)
            def _():
                swap_w(wd_ref, wd, wds, wdr, 2 * (t - NP)).start()
                swap_w(wd_ref, wd, wds, wdr, 2 * (t - NP) + 1).start()

        @pl.when(jnp.logical_and(t >= 1, t - 1 < NI))
        def _():
            j = t - 1
            d1(j, 0).wait_recv()
            d2(j, 0).start()
            d1(j, 1).wait_recv()
            d2(j, 1).start()

        @pl.when(jnp.logical_and(t >= 2, t - 2 < NI))
        def _():
            j = t - 2
            d2(j, 0).wait_recv()
            d2(j, 1).wait_recv()
            d3(j).start()

        @pl.when(jnp.logical_and(t >= 3, t - 3 < NI))
        def _():
            j = t - 3
            d3(j).wait_recv()
            d4(j).start()

        @pl.when(jnp.logical_and(t >= 4, t - 4 < NI))
        def _():
            j = t - 4
            d4(j).wait_recv()

            @pl.when(j < ZP)
            def _():
                d5(j, 0).start()
                d5(j, 1).start()

            gate(item(j))

        @pl.when(jnp.logical_and(t >= 9, t - 9 < ZP))
        def _():
            j = t - 9
            s = other(j)
            load_tok(s, 0).wait()
            load_tok(s, 1).wait()
            d5(j, 0).wait_recv()
            d5(j, 1).wait_recv()
            gate(s)

        return 0

    lax.fori_loop(0, 13, g_tick, 0)

    def g_drain(j, _):
        for d in range(2):
            d1(j, d).wait_send()
            d2(j, d).wait_send()
        d3(j).wait_send()
        d4(j).wait_send()

        @pl.when(j < ZP)
        def _():
            d5(j, 0).wait_send()
            d5(j, 1).wait_send()

        return 0

    wait_wt()
    own = 2 * (e // 2) + k
    col = lax.broadcasted_iota(jnp.int32, (EXPERTS, FF2), 1)
    row = lax.broadcasted_iota(jnp.int32, (EXPERTS, FF2), 0)
    named = jnp.where(col < FF, own, own + 1 - 2 * k)
    sel = jnp.where(row == named, 1.0, 0.0).astype(F32)

    @pl.loop(0, 8)
    def _(b):
        rows = pl.ds(pl.multiple_of(b * ROWS, ROWS), ROWS)
        v = pre[rows, :]
        scale = lax.dot_general(
            wt[b], sel, (((0,), (0,)), ((), ())),
            preferred_element_type=F32, precision=lax.Precision.HIGHEST,
        )
        hid[rows, :] = (scale * (v / (1.0 + jnp.exp(-v)))).astype(BF)

    lax.fori_loop(0, NI, g_drain, 0)

    def down(s):
        load_w(wd_ref, wd, wdo, s).wait()
        swap_w(wd_ref, wd, wds, wdr, s).wait_recv()

        @pl.loop(0, 4)
        def _(i):
            rows = pl.ds(pl.multiple_of(i * 256, 256), 256)
            r = jnp.dot(hid[rows, :], wd[s], preferred_element_type=F32).astype(BF)
            for h in range(2):
                xp[s, h, i // 2, pl.ds((i % 2) * 2, 2)] = r[:, h * HW:(h + 1) * HW].reshape(2, ROWS, HW)

    def total(*parts):
        acc = parts[0].astype(F32)
        for part in parts[1:]:
            acc = acc + part.astype(F32)
        return acc

    top, low = pl.ds(0, 64), pl.ds(64, 64)

    def a1(p, d):
        return remote(xp.at[2 * p, d, :, 2], ry1.at[p, d], y1s.at[p, d], y1r.at[p, d], yp if d == 0 else ym)

    def a2(p, d):
        return remote(
            xp.at[2 * p, :, :, 1 if d == 0 else 3], ry2.at[p, d],
            y2s.at[p, d], y2r.at[p, d], yp if d == 0 else ym,
        )

    def a3(p, d):
        return remote(
            xp.at[2 * p, lo, 1, 0, top if d == 0 else low], rx1.at[p, d],
            x1s.at[p, d], x1r.at[p, d], inner if d == 0 else outer,
        )

    def a4(p, d):
        return remote(
            xp.at[2 * p, ol, d, 0], rx2.at[p, d],
            x2s.at[p, d], x2r.at[p, d], inner if d == 0 else outer,
        )

    def b1(p, d):
        return remote(
            xp.at[2 * p + 1, lo, 1, :, top if d == 0 else low], qx1.at[p, d],
            u1s.at[p, d], u1r.at[p, d], inner if d == 0 else outer,
        )

    def b2(p, d):
        return remote(
            xp.at[2 * p + 1, ol, d], qx2.at[p, d],
            u2s.at[p, d], u2r.at[p, d], inner if d == 0 else outer,
        )

    def b3(p, d):
        return remote(
            xp.at[2 * p + 1, lo, 0, 2, top if d == 0 else low], qy1.at[p, d],
            v1s.at[p, d], v1r.at[p, d], yp if d == 0 else ym,
        )

    def b4(p, d):
        return remote(
            xp.at[2 * p + 1, lo, 0, 1 if d == 0 else 3], qy2.at[p, d],
            v2s.at[p, d], v2r.at[p, d], yp if d == 0 else ym,
        )

    def z1(s):
        for dz in range(1, 8):
            remote(
                tz.at[s, (z + dz) % 8], tz.at[s, 8 + (7 - dz)], z1s.at[s], z1r.at[s], zdev(dz, lo)
            ).start()

    def z1_done(s):
        got = tz.at[s, pl.ds(8, 7)]
        return remote(got, got, z1s.at[s], z1r.at[s], core)

    def place(s):
        return o_ref.at[
            pl.ds(pl.multiple_of(z * 16, 16), 16),
            pl.ds(pl.multiple_of(s * CW + lo * HW, HW), HW),
        ]

    def keep(s):
        return pltpu.make_async_copy(fz.at[s], place(s), aglo.at[s])

    def z2(s):
        keep(s).start()
        for dz in range(8):
            if dz:
                remote(fz.at[s], place(s), ags.at[s], agr.at[s], zdev(dz, lo)).start()
            remote(fz.at[s], place(s), ags.at[s], agr.at[s], zdev(dz, ol)).start()

    def z2_done(s):
        return remote(tz.at[s], tz.at[s], ags.at[s], agr.at[s], core)

    def both(fn, p, what):
        for d in range(2):
            cp = fn(p, d)
            getattr(cp, what)()

    def at_stage(t, n):
        return jnp.logical_and(t >= n, t - n < NP)

    def s_tick(t, _):
        @pl.when(t < NP)
        def _():
            down(2 * t)
            both(a1, t, "start")
            down(2 * t + 1)
            both(b1, t, "start")

        @pl.when(at_stage(t, 1))
        def _():
            p = t - 1
            s = 2 * p
            both(a1, p, "wait_recv")
            xp[s, 0, :, 1] = total(xp[s, 0, :, 1], ry1[p, 0]).astype(BF)
            a2(p, 0).start()
            xp[s, 1, :, 3] = total(xp[s, 1, :, 3], ry1[p, 1]).astype(BF)
            a2(p, 1).start()
            s = 2 * p + 1
            both(b1, p, "wait_recv")
            xp[s, ol, 1, :, 0:64] = total(xp[s, ol, 1, :, 0:64], qx1[p, 0]).astype(BF)
            b2(p, 1).start()
            xp[s, ol, 0, :, 64:128] = total(xp[s, ol, 0, :, 64:128], qx1[p, 1]).astype(BF)
            b2(p, 0).start()

        @pl.when(at_stage(t, 2))
        def _():
            p = t - 2
            s = 2 * p
            both(a2, p, "wait_recv")
            for h in range(2):
                xp[s, h, :, 0] = total(xp[s, h, :, 0], ry2[p, 0, h], ry2[p, 1, h]).astype(BF)
            both(a3, p, "start")
            s = 2 * p + 1
            both(b2, p, "wait_recv")
            xp[s, lo, 0] = total(xp[s, lo, 0], qx2[p, 0], qx2[p, 1]).astype(BF)
            both(b3, p, "start")

        @pl.when(at_stage(t, 3))
        def _():
            p = t - 3
            s = 2 * p
            both(a3, p, "wait_recv")
            xp[s, ol, 1, 0, 0:64] = total(xp[s, ol, 1, 0, 0:64], rx1[p, 0]).astype(BF)
            a4(p, 1).start()
            xp[s, ol, 0, 0, 64:128] = total(xp[s, ol, 0, 0, 64:128], rx1[p, 1]).astype(BF)
            a4(p, 0).start()
            s = 2 * p + 1
            both(b3, p, "wait_recv")
            xp[s, lo, 0, 1, 0:64] = total(xp[s, lo, 0, 1, 0:64], qy1[p, 0]).astype(BF)
            b4(p, 0).start()
            xp[s, lo, 0, 3, 64:128] = total(xp[s, lo, 0, 3, 64:128], qy1[p, 1]).astype(BF)
            b4(p, 1).start()

        @pl.when(at_stage(t, 4))
        def _():
            p = t - 4
            s = 2 * p
            both(a4, p, "wait_recv")
            tz[s, 0:8] = total(xp[s, lo, 0, 0], rx2[p, 0], rx2[p, 1]).astype(BF).reshape(8, 16, HW)
            z1(s)
            s = 2 * p + 1
            both(b4, p, "wait_recv")
            tz[s, 0:8] = total(xp[s, lo, 0, 0], qy2[p, 0], qy2[p, 1]).astype(BF).reshape(8, 16, HW)
            z1(s)

        @pl.when(at_stage(t, 5))
        def _():
            p = t - 5
            for q in range(2):
                s = 2 * p + q
                z1_done(s).wait_recv()
                acc = tz[s, z].astype(F32)
                for i in range(7):
                    acc = acc + tz[s, 8 + i].astype(F32)
                fz[s] = acc.astype(BF)
                z2(s)

        return 0

    lax.fori_loop(0, NP + 5, s_tick, 0)

    def s_drain(p, _):
        for fn in (a1, a2, a3, a4, b1, b2, b3, b4):
            both(fn, p, "wait_send")
        for q in range(2):
            s = 2 * p + q
            swap_w(wg_ref, wg, wgs, wgr, s).wait_send()
            swap_w(wd_ref, wd, wds, wdr, s).wait_send()
            z1_done(s).wait_send()
            keep(s).wait()
            z2_done(s).wait_send()
            z2_done(s).wait_recv()
        return 0

    lax.fori_loop(0, NP, s_drain, 0)


def on_device(tokens, routes, route_weights, w_gate, w_down):
    ids = jnp.arange(EXPERTS, dtype=jnp.int32)[:, None, None]
    wt = jnp.sum(jnp.where(routes.T[None] == ids, route_weights.T[None], 0.0), 1)
    dma = pltpu.SemaphoreType.DMA
    sems = (
        [dma((NS, 2))] + [dma((NS,))] * 6 + [dma, dma]
        + [dma((NI, 2))] * 4 + [dma((NI,))] * 4 + [dma((ZP, 2))] * 2
        + [dma((NP, 2))] * 16 + [dma((NS,))] * 5
    )
    return pl.pallas_call(
        kernel,
        out_shape=jax.ShapeDtypeStruct((ROWS, D), BF),
        in_specs=[pl.BlockSpec(memory_space=pltpu.VMEM)] + [pl.BlockSpec(memory_space=pl.ANY)] * 3,
        out_specs=pl.BlockSpec(memory_space=pl.ANY),
        scratch_shapes=[
            pltpu.VMEM((NS, 2, 2, 4, ROWS, HW), BF),
            pltpu.VMEM((NS, FF2, CW), BF),
            pltpu.VMEM((NS, FF2, CW), BF),
            pltpu.VMEM((8 * ROWS, FF2), F32),
            pltpu.VMEM((8 * ROWS, FF2), BF),
            pltpu.VMEM((8, EXPERTS, ROWS), F32),
            pltpu.VMEM((NP, 2, 2, ROWS, HW), BF),
            pltpu.VMEM((NP, 2, 2, 2, ROWS, HW), BF),
            pltpu.VMEM((NP, 2, 64, HW), BF),
            pltpu.VMEM((NP, 2, ROWS, HW), BF),
            pltpu.VMEM((NP, 2, 4, 64, HW), BF),
            pltpu.VMEM((NP, 2, 4, ROWS, HW), BF),
            pltpu.VMEM((NP, 2, 64, HW), BF),
            pltpu.VMEM((NP, 2, ROWS, HW), BF),
            pltpu.VMEM((NS, 15, 16, HW), BF),
            pltpu.VMEM((NS, 16, HW), BF),
        ] + sems,
        compiler_params=pltpu.CompilerParams(
            collective_id=0, has_side_effects=True, vmem_limit_bytes=56 << 20
        ),
        cost_estimate=pl.CostEstimate(
            flops=4 * 8 * ROWS * FF2 * D, bytes_accessed=4 * FF * D * 2, transcendentals=8 * ROWS * FF2
        ),
        name="moe",
    )(wt, tokens, w_gate, w_down)


def solution(mesh):
    in_specs = (
        P("expert", None),
        P("expert", None),
        P("expert", None),
        P("expert", "cuts", None),
        P("expert", "cuts", None),
    )
    return jax.shard_map(
        on_device, mesh=mesh, in_specs=in_specs, out_specs=P("expert", None), check_vma=False
    )
```

time: 799 us -> 194 us (0.24)
  waiting for transfers between devices: 691 us -> 0 us
  Pallas kernels: 0 us -> 190 us
  local copies, waits for them, and re-layouts: 47.8 us -> 2.69 us
  blocking collectives: 21.1 us -> 0 us
  matrix products: 16.7 us -> 0 us
  between operations: 13.2 us -> 0.01 us
    reduce_scatter x1 -> x0, waiting for transfers between devices: 270 us -> none  [on_device(): lax.psum_scatter(cut_terms.astype(jnp.bfloat16), 'cuts', scatter_dimensio...]
    all_gather x1 -> x0, waiting for transfers between devices: 265 us -> none  [on_device(): piece = lax.all_gather(arrived, 'cuts', axis=1, tiled=True)]
    pallas_call x0 -> x1, Pallas kernels: none -> 190 us  [on_device(): pl.pallas_call(kernel, out_shape=jax.ShapeDtypeStruct((ROWS, D), BF), in_...]
    psum x1 -> x0, waiting for transfers between devices: 140 us -> none  [on_device(): mixed = lax.psum(slot_part.astype(jnp.bfloat16), 'cuts')]
    convert_element_type x2 -> x0, local copies, waits for them, and re-layouts: 27.2 us -> none  [the longest x1 26.9 us: on_device(): cut_terms.astype(jnp.bfloat16)]
    all_to_all x1 -> x0, blocking collectives: 21.1 us -> none  [on_device(): lax.all_to_all(outgoing, 'expert', split_axis=0, concat_axis=0, tiled=True)]
    dot_general x4 -> x0, matrix products: 16.7 us -> none  [the longest x1 9.1 us: on_device(): jnp.einsum('rcf,fd->rcd', hidden, down_rows, preferred_element_type=jnp.f...]
    all_to_all x1 -> x0, waiting for transfers between devices: 15.1 us -> none  [on_device(): lax.all_to_all(summed, 'expert', split_axis=0, concat_axis=0, tiled=True)]
  transfers between devices with their start and end apart: 4 -> 0, of which waited for: 4 -> 0; matrix products, arithmetic and copies ran while one was open for 0% -> 0% of each run, Pallas kernels for 0% -> 0%
where the time goes in v1:
time: 194 us
  Pallas kernels  190 us (98%)
  local copies, waits for them, and re-layouts  2.69 us (1%)
    pallas_call x1, Pallas kernels, on_device(): pl.pallas_call(kernel, out_shape=jax.ShapeDtypeStruct((ROWS, D), BF), in_...  190 us

profile of v1, /device:TPU:2, one launch (start us, length us, event | category | flops | bytes accessed | tf_op | source)
XLA Modules:
  0.0 194.0 jit_solution(6517612105285426721)
XLA Ops:
  0.0 1.3 select_reduce_fusion.wt_ref
  1.3 190.0 %moe.1 = bf16[128,6144]{1,0:T(8,128)(2,1)} custom-call(f32[16,128]{1,0:T(8,128)} %select_reduce_fusion.wt_ref, bf16[128,6144]{1,0:T(8,128)(2,1)} %tok_ref.1, bf16[1,336,6144]{2,1,0:T(8,128)(2,1)} %wg_ref.1, bf16[1,336,6144]{2,1,0:T(8,128)(2,1)} %wd_ref.1), custom_call_target="tpu_custom_call" | custom-call | flops 16911433728 | bytes 16515072 | tf_op jit(solution)/shard_map/moe/pallas_call | solution.py:483
  191.3 2.7 %copy.7 = bf16[128,6144]{1,0:T(8,128)(2,1)} copy(bf16[128,6144]{1,0:T(8,128)(2,1)} %moe.1) | data formatting | bytes 3145728

commit v2 on v0

v2 whole, which is shorter than its diff:
```python
import jax
import jax.numpy as jnp
from jax import lax
from jax.experimental import pallas as pl
from jax.experimental.pallas import tpu as pltpu
from jax.sharding import PartitionSpec as P

MESH = pl.DeviceIdType.MESH
BF = jnp.bfloat16
F32 = jnp.float32

D = 6144
HALF = D // 2
FF = 336
FFP = 384
PAIR = 2 * FFP
ROWS = 128
EXPERTS = 16
NS = 6
CW = HALF // NS
HW = CW // 2
NJ = 2 * NS
RSLOT = {0: 0, 1: 1, 3: 2, 2: 3}


def kernel(
    wt_ref, tok_ref, wg_ref, wd_ref, o_ref,
    xp, pb, wg, wd, pre, es, er, hid, wt,
    ry1, ry2, rx1, rx2, tz, fz,
    tok_sem,
    wgo, wgs, wgr, wgzs, wgzr, wgls, wglr,
    wdo, wds, wdr, wdzs, wdzr, wdls, wdlr,
    wts, wtr,
    s1s, s1r, s2s, s2r, os_, or_, is_, ir_, exs, exr,
    y1s, y1r, y2s, y2r, x1s, x1r, x2s, x2r,
    z1s, z1r, ags, agr, aglo,
):
    e = lax.axis_index("expert")
    c = lax.axis_index("cuts")
    hi, y, k = e // 8, (e // 2) % 4, e % 2
    z, lo = c // 2, c % 2
    ol = 1 - lo
    zpar, zi = z % 2, z // 2

    def dev(hi_, y_, k_, z_, lo_):
        return (hi_ * 8 + y_ * 2 + k_, z_ * 2 + lo_)

    yp = dev(hi, (y + 1) % 4, k, z, lo)
    ym = dev(hi, (y + 3) % 4, k, z, lo)
    inner = dev(hi, y, k, z, ol)
    outer = dev(1 - hi, y, k, z, ol)
    core = dev(hi, y, 1 - k, z, lo)

    def zdev(dz, lo_):
        return dev(hi, y, k, (z + dz + 8) % 8, lo_)

    def rel(dx, dy):
        if dx == 0:
            return dev(hi, (y + dy) % 4, k, z, lo)
        return dev(1 - hi, (y + dy) % 4, k, z, ol)

    def remote(src, dst, ss, rs, to):
        return pltpu.make_async_remote_copy(
            src_ref=src, dst_ref=dst, send_sem=ss, recv_sem=rs, device_id=to, device_id_type=MESH
        )

    def cols(par, s):
        return pl.ds(pl.multiple_of(par * HALF + s * CW, CW), CW)

    def load_tok(s, h):
        at = pl.multiple_of(zpar * HALF + s * CW + h * HW, HW)
        return pltpu.make_async_copy(tok_ref.at[:, pl.ds(at, HW)], xp.at[s, h, 0, 0], tok_sem.at[s, h])

    real = pl.ds(0, FF)
    own_q, far_q = 3 * k, 2 - k

    class Weights:
        def __init__(self, src, dst, so, ss, sr, zs, zr, ls, lr):
            self.src, self.dst = src, dst
            self.so, self.ss, self.sr, self.zs, self.zr, self.ls, self.lr = so, ss, sr, zs, zr, ls, lr

        def local(self, s):
            return pltpu.make_async_copy(
                self.src.at[0, :, cols(zpar, s)], self.dst.at[s, own_q, real], self.so.at[s]
            )

        def swap(self, s):
            return remote(
                self.src.at[0, :, cols(zpar, s)], self.dst.at[s, own_q, real], self.ss.at[s], self.sr.at[s], core
            )

        def along(self, s):
            return remote(
                self.src.at[0, :, cols(1 - zpar, s)], self.dst.at[s, far_q, real],
                self.zs.at[s], self.zr.at[s], zdev(1 - 2 * k, lo),
            )

        def relay(self, s):
            ref = self.dst.at[s, far_q, real]
            return remote(ref, ref, self.ls.at[s], self.lr.at[s], core)

        def ready(self, s):
            self.local(s).wait()
            self.swap(s).wait_recv()
            self.relay(s).wait_recv()

        def drain(self, s):
            self.swap(s).wait_send()
            self.along(s).wait_send()
            self.relay(s).wait_send()

    gw = Weights(wg_ref, wg, wgo, wgs, wgr, wgzs, wgzr, wgls, wglr)
    dw = Weights(wd_ref, wd, wdo, wds, wdr, wdzs, wdzr, wdls, wdlr)

    def loop(n, body):
        def step(i, _):
            body(i)
            return 0

        lax.fori_loop(0, n, step, 0)

    def start_tok(s):
        load_tok(s, 0).start()
        load_tok(s, 1).start()

    def start_local(s):
        gw.local(s).start()
        dw.local(s).start()

    loop(NS, start_tok)

    bar = pltpu.get_barrier_semaphore()
    partners = [core]
    for dx in range(2):
        for dy in range(4):
            if (dx, dy) != (0, 0):
                partners.append(rel(dx, dy))
    for dz in range(8):
        if dz:
            partners.append(zdev(dz, lo))
        partners.append(zdev(dz, ol))
    for p in partners:
        pl.semaphore_signal(bar, inc=1, device_id=p, device_id_type=MESH)
    loop(NS, start_local)
    wt[0] = wt_ref[...]

    def clear_pad(s):
        for q in range(4):
            wg[s, q, FF:FFP, :] = jnp.zeros((FFP - FF, CW), BF)
            wd[s, q, FF:FFP, :] = jnp.zeros((FFP - FF, CW), BF)

    loop(NS, clear_pad)
    pl.semaphore_wait(bar, len(partners))

    def s1(j, d):
        return remote(
            xp.at[j, :, 0, 0], xp.at[j, :, 0, 2 - d], s1s.at[j, d], s1r.at[j, d], yp if d == 0 else ym
        )

    def s2(j, d):
        return remote(
            xp.at[j, d, 0, 2 - d], xp.at[j, d, 0, 3], s2s.at[j, d], s2r.at[j, d], yp if d == 0 else ym
        )

    part = (pl.ds(0, 1), pl.ds(1, 2), pl.ds(3, 1))

    def og(j, n):
        return remote(xp.at[j, lo, 0, part[n]], xp.at[j, lo, 1, part[n]], os_.at[j, n], or_.at[j, n], outer)

    def ig(j, n):
        ref = xp.at[j, ol, 1, part[n]]
        return remote(ref, ref, is_.at[j, n], ir_.at[j, n], inner)

    def gate(j, dx, r0, nr):
        m = nr * ROWS
        row0 = (dx * 4 + r0) * ROWS

        @pl.loop(0, 2)
        def _(i):
            acc = pre[i, row0:row0 + m, :]
            for h in range(2):
                xs = xp[j, h, dx, r0:r0 + nr].reshape(m, HW)
                ws = wg[j, pl.ds(2 * i, 2), :, h * HW:(h + 1) * HW].reshape(PAIR, HW)
                acc = acc + lax.dot_general(xs, ws, (((1,), (1,)), ((), ())), preferred_element_type=F32)
            pre[i, row0:row0 + m, :] = acc

    def ex(n, d):
        rows = (pl.ds(0, 384), pl.ds(384, 128), pl.ds(512, 512))[n]
        return remote(es.at[d, rows], er.at[d, rows], exs.at[n, d], exr.at[n, d], zdev(1 - 2 * d, lo))

    def exchange(n):
        b0, nb = ((0, 3), (3, 1), (4, 4))[n]

        def stage(b):
            rows = pl.ds(pl.multiple_of((b0 + b) * ROWS, ROWS), ROWS)
            for d in range(2):
                es[d, rows, :] = pre[d, rows, :].astype(BF)

        loop(nb, stage)
        ex(n, 0).start()
        ex(n, 1).start()

    def first(j):
        gw.along(j).start()
        gw.swap(j).start()

    loop(NS, first)

    def l0(j):
        load_tok(j, 0).wait()
        load_tok(j, 1).wait()
        s1(j, 0).start()
        s1(j, 1).start()
        og(j, 0).start()

    loop(NS, l0)
    for dx in range(2):
        for dy in range(4):
            if (dx, dy) != (0, 0):
                remote(wt_ref, wt.at[dx * 4 + RSLOT[(4 - dy) % 4]], wts, wtr, rel(dx, dy)).start()
    dw.along(0).start()

    def clear_pre(b):
        rows = pl.ds(pl.multiple_of(b * ROWS, ROWS), ROWS)
        for i in range(2):
            pre[i, rows, :] = jnp.zeros((ROWS, PAIR), F32)

    loop(8, clear_pre)

    def l1(t):
        @pl.when(t < NS)
        def _():
            s1(t, 0).wait_recv()
            s2(t, 0).start()
            s1(t, 1).wait_recv()
            s2(t, 1).start()
            og(t, 1).start()
            og(t, 0).wait_recv()
            ig(t, 0).start()
            gw.along(t).wait_recv()
            gw.relay(t).start()

        @pl.when(jnp.logical_and(t >= 2, t < NS))
        def _():
            og(t - 2, 1).wait_recv()
            ig(t - 2, 1).start()

        @pl.when(t >= 1)
        def _():
            gw.ready(t - 1)
            gate(t - 1, 0, 0, 3)

    loop(NS + 1, l1)
    exchange(0)

    def l2(j):
        s2(j, 0).wait_recv()
        s2(j, 1).wait_recv()
        og(j, 2).start()

        @pl.when(j < 2)
        def _():
            og(j + 4, 1).wait_recv()
            ig(j + 4, 1).start()

        dw.swap(j).start()
        gate(j, 0, 3, 1)

    loop(NS, l2)
    exchange(1)
    dw.along(1).start()

    def l3(t):
        @pl.when(t < NS)
        def _():
            og(t, 2).wait_recv()
            ig(t, 2).start()

        @pl.when(t >= 2)
        def _():
            for n in range(3):
                ig(t - 2, n).wait_recv()
            gate(t - 2, 1, 0, 4)

    loop(NS + 2, l3)
    exchange(2)

    def more(s):
        dw.along(s + 2).start()

    loop(NS - 2, more)

    def relay_down(s):
        dw.along(s).wait_recv()
        dw.relay(s).start()

    relay_down(0)

    got = wt.at[pl.ds(1, 7)]
    all_wt = remote(got, got, wts, wtr, core)
    all_wt.wait_send()
    all_wt.wait_recv()
    col = lax.broadcasted_iota(jnp.int32, (EXPERTS, PAIR), 1)
    row = lax.broadcasted_iota(jnp.int32, (EXPERTS, PAIR), 0)
    e0 = 2 * (e // 2)
    hit0 = jnp.logical_and(row == e0, col < FF)
    hit1 = jnp.logical_and(row == e0 + 1, jnp.logical_and(col >= FFP, col < FFP + FF))
    sel = jnp.where(jnp.logical_or(hit0, hit1), 1.0, 0.0).astype(F32)

    def hidden(b):
        rows = pl.ds(pl.multiple_of(b * ROWS, ROWS), ROWS)
        scale = lax.dot_general(
            wt[b], sel, (((0,), (0,)), ((), ())),
            preferred_element_type=F32, precision=lax.Precision.HIGHEST,
        )
        for i in range(2):
            v = pre[i, rows, :] + er[1 - i, rows, :].astype(F32)
            hid[rows, i * PAIR:(i + 1) * PAIR] = (scale * (v / (1.0 + jnp.exp(-v)))).astype(BF)

    for n in range(2):
        ex(n, 0).wait_recv()
        ex(n, 1).wait_recv()
    loop(4, hidden)
    relay_down(1)

    def down(s, dx):
        @pl.loop(0, 2)
        def _(i):
            rows = pl.ds(pl.multiple_of(dx * 512 + i * 256, 256), 256)
            r = jnp.dot(hid[rows, :], wd[s].reshape(4 * FFP, CW), preferred_element_type=F32).astype(BF)
            for h in range(2):
                pb[s, h, dx, pl.ds(i * 2, 2)] = r[:, h * HW:(h + 1) * HW].reshape(2, ROWS, HW)

    def total(*parts):
        acc = parts[0].astype(F32)
        for p in parts[1:]:
            acc = acc + p.astype(F32)
        return acc.astype(BF)

    top, low = pl.ds(0, 64), pl.ds(64, 64)

    def a1(s, dx, d):
        return remote(pb.at[s, d, dx, 3], ry1.at[s, dx, d], y1s.at[s, dx, d], y1r.at[s, dx, d], yp if d == 0 else ym)

    def a2(s, dx, d):
        return remote(
            pb.at[s, :, dx, 1 + d], ry2.at[s, dx, d], y2s.at[s, dx, d], y2r.at[s, dx, d], yp if d == 0 else ym
        )

    def a3(s, d):
        return remote(
            pb.at[s, lo, 1, 0, top if d == 0 else low], rx1.at[s, d],
            x1s.at[s, d], x1r.at[s, d], inner if d == 0 else outer,
        )

    def a4(s, d):
        return remote(
            pb.at[s, ol, d, 0], rx2.at[s, d], x2s.at[s, d], x2r.at[s, d], inner if d == 0 else outer
        )

    def z1(s):
        for dz in range(1, 4):
            remote(
                tz.at[s, (zi + dz) % 4], tz.at[s, 4 + (3 - dz)], z1s.at[s], z1r.at[s], zdev(2 * dz, lo)
            ).start()

    def z1_done(s):
        ref = tz.at[s, pl.ds(4, 3)]
        return remote(ref, ref, z1s.at[s], z1r.at[s], core)

    def place(s):
        return o_ref.at[
            pl.ds(pl.multiple_of(zi * 32, 32), 32),
            pl.ds(pl.multiple_of(zpar * HALF + s * CW + lo * HW, HW), HW),
        ]

    def keep(s):
        return pltpu.make_async_copy(fz.at[s], place(s), aglo.at[s])

    def z2(s):
        keep(s).start()
        for dz in range(8):
            if dz:
                remote(fz.at[s], place(s), ags.at[s], agr.at[s], zdev(dz, lo)).start()
            remote(fz.at[s], place(s), ags.at[s], agr.at[s], zdev(dz, ol)).start()

    def z2_done(s):
        return remote(tz.at[s], tz.at[s], ags.at[s], agr.at[s], core)

    def job(t):
        early = t < 4
        return jnp.where(early, t % 2, t // 2), jnp.where(early, t // 2, t % 2)

    def r_tick(t):
        @pl.when(t == 2)
        def _():
            ex(2, 0).wait_recv()
            ex(2, 1).wait_recv()

            def late(b):
                hidden(b + 4)

            loop(4, late)

        @pl.when(t < NJ)
        def _():
            s, dx = job(t)

            @pl.when(dx == 0)
            def _():
                dw.ready(s)

            down(s, dx)
            a1(s, dx, 0).start()
            a1(s, dx, 1).start()

        @pl.when(jnp.logical_and(t >= 1, t - 1 < NJ))
        def _():
            s, dx = job(t - 1)
            for d in range(2):
                a1(s, dx, d).wait_recv()
                pb[s, d, dx, 1 + d] = total(pb[s, d, dx, 1 + d], ry1[s, dx, d])
                a2(s, dx, d).start()

        @pl.when(jnp.logical_and(t >= 2, t - 2 < NJ))
        def _():
            s, dx = job(t - 2)
            a2(s, dx, 0).wait_recv()
            a2(s, dx, 1).wait_recv()
            pb[s, :, dx, 0] = total(pb[s, :, dx, 0], ry2[s, dx, 0], ry2[s, dx, 1])

        def stage(n, fn):
            @pl.when(jnp.logical_and(t % 2 == n % 2, jnp.logical_and(t >= n, t - n < NJ)))
            def _():
                fn((t - n) // 2)

        def go_x1(s):
            a3(s, 0).start()
            a3(s, 1).start()

        def go_x2(s):
            a3(s, 0).wait_recv()
            pb[s, ol, 1, 0, 0:64] = total(pb[s, ol, 1, 0, 0:64], rx1[s, 0])
            a4(s, 1).start()
            a3(s, 1).wait_recv()
            pb[s, ol, 0, 0, 64:128] = total(pb[s, ol, 0, 0, 64:128], rx1[s, 1])
            a4(s, 0).start()

        def go_z1(s):
            a4(s, 0).wait_recv()
            a4(s, 1).wait_recv()
            tz[s, 0:4] = total(pb[s, lo, 0, 0], rx2[s, 0], rx2[s, 1]).reshape(4, 32, HW)
            z1(s)

        def go_z2(s):
            z1_done(s).wait_recv()
            fz[s] = total(tz[s, zi], tz[s, 4], tz[s, 5], tz[s, 6])
            z2(s)

        stage(4, go_x1)
        stage(5, go_x2)
        stage(6, go_z1)
        stage(7, go_z2)

        @pl.when(jnp.logical_and(t % 2 == 1, jnp.logical_and(t >= 3, t < NJ - 1)))
        def _():
            relay_down((t + 1) // 2)

    loop(NJ + 6, r_tick)

    def drain(s):
        gw.drain(s)
        dw.drain(s)
        for d in range(2):
            s1(s, d).wait_send()
            s2(s, d).wait_send()
            a3(s, d).wait_send()
            a4(s, d).wait_send()
            for dx in range(2):
                a1(s, dx, d).wait_send()
                a2(s, dx, d).wait_send()
        for n in range(3):
            og(s, n).wait_send()
            ig(s, n).wait_send()
        z1_done(s).wait_send()
        keep(s).wait()
        z2_done(s).wait_send()
        z2_done(s).wait_recv()

    loop(NS, drain)
    for n in range(3):
        ex(n, 0).wait_send()
        ex(n, 1).wait_send()


def on_device(tokens, routes, route_weights, w_gate, w_down):
    ids = jnp.arange(EXPERTS, dtype=jnp.int32)[:, None, None]
    wt = jnp.sum(jnp.where(routes.T[None] == ids, route_weights.T[None], 0.0), 1)
    dma = pltpu.SemaphoreType.DMA
    sems = (
        [dma((NS, 2))] + [dma((NS,))] * 14 + [dma, dma]
        + [dma((NS, 2))] * 4 + [dma((NS, 3))] * 4 + [dma((3, 2))] * 2
        + [dma((NS, 2, 2))] * 4 + [dma((NS, 2))] * 4 + [dma((NS,))] * 5
    )
    return pl.pallas_call(
        kernel,
        out_shape=jax.ShapeDtypeStruct((ROWS, D), BF),
        in_specs=[pl.BlockSpec(memory_space=pltpu.VMEM)] + [pl.BlockSpec(memory_space=pl.ANY)] * 3,
        out_specs=pl.BlockSpec(memory_space=pl.ANY),
        scratch_shapes=[
            pltpu.VMEM((NS, 2, 2, 4, ROWS, HW), BF),
            pltpu.VMEM((NS, 2, 2, 4, ROWS, HW), BF),
            pltpu.VMEM((NS, 4, FFP, CW), BF),
            pltpu.VMEM((NS, 4, FFP, CW), BF),
            pltpu.VMEM((2, 8 * ROWS, PAIR), F32),
            pltpu.VMEM((2, 8 * ROWS, PAIR), BF),
            pltpu.VMEM((2, 8 * ROWS, PAIR), BF),
            pltpu.VMEM((8 * ROWS, 2 * PAIR), BF),
            pltpu.VMEM((8, EXPERTS, ROWS), F32),
            pltpu.VMEM((NS, 2, 2, ROWS, HW), BF),
            pltpu.VMEM((NS, 2, 2, 2, ROWS, HW), BF),
            pltpu.VMEM((NS, 2, 64, HW), BF),
            pltpu.VMEM((NS, 2, ROWS, HW), BF),
            pltpu.VMEM((NS, 15, 32, HW), BF),
            pltpu.VMEM((NS, 32, HW), BF),
        ] + sems,
        compiler_params=pltpu.CompilerParams(
            collective_id=0, has_side_effects=True, vmem_limit_bytes=58 << 20
        ),
        cost_estimate=pl.CostEstimate(
            flops=8 * 8 * ROWS * FF * D, bytes_accessed=4 * FF * D * 2, transcendentals=32 * ROWS * FF
        ),
        name="moe",
    )(wt, tokens, w_gate, w_down)


def solution(mesh):
    in_specs = (
        P("expert", None),
        P("expert", None),
        P("expert", None),
        P("expert", "cuts", None),
        P("expert", "cuts", None),
    )
    return jax.shard_map(
        on_device, mesh=mesh, in_specs=in_specs, out_specs=P("expert", None), check_vma=False
    )
```

time: 799 us -> 173 us (0.22)
  waiting for transfers between devices: 691 us -> 0 us
  Pallas kernels: 0 us -> 168 us
  local copies, waits for them, and re-layouts: 47.8 us -> 2.69 us
  blocking collectives: 21.1 us -> 0 us
  matrix products: 16.7 us -> 0 us
  between operations: 13.2 us -> 0.01 us
    reduce_scatter x1 -> x0, waiting for transfers between devices: 270 us -> none  [on_device(): lax.psum_scatter(cut_terms.astype(jnp.bfloat16), 'cuts', scatter_dimensio...]
    all_gather x1 -> x0, waiting for transfers between devices: 265 us -> none  [on_device(): piece = lax.all_gather(arrived, 'cuts', axis=1, tiled=True)]
    pallas_call x0 -> x1, Pallas kernels: none -> 168 us  [on_device(): pl.pallas_call(kernel, out_shape=jax.ShapeDtypeStruct((ROWS, D), BF), in_...]
    psum x1 -> x0, waiting for transfers between devices: 140 us -> none  [on_device(): mixed = lax.psum(slot_part.astype(jnp.bfloat16), 'cuts')]
    convert_element_type x2 -> x0, local copies, waits for them, and re-layouts: 27.2 us -> none  [the longest x1 26.9 us: on_device(): cut_terms.astype(jnp.bfloat16)]
    all_to_all x1 -> x0, blocking collectives: 21.1 us -> none  [on_device(): lax.all_to_all(outgoing, 'expert', split_axis=0, concat_axis=0, tiled=True)]
    dot_general x4 -> x0, matrix products: 16.7 us -> none  [the longest x1 9.1 us: on_device(): jnp.einsum('rcf,fd->rcd', hidden, down_rows, preferred_element_type=jnp.f...]
    all_to_all x1 -> x0, waiting for transfers between devices: 15.1 us -> none  [on_device(): lax.all_to_all(summed, 'expert', split_axis=0, concat_axis=0, tiled=True)]
  transfers between devices with their start and end apart: 4 -> 0, of which waited for: 4 -> 0; matrix products, arithmetic and copies ran while one was open for 0% -> 0% of each run, Pallas kernels for 0% -> 0%
where the time goes in v2:
time: 173 us; the launch traced here: 172 us
  Pallas kernels  168 us (97%)
  local copies, waits for them, and re-layouts  2.69 us (2%)
    pallas_call x1, Pallas kernels, on_device(): pl.pallas_call(kernel, out_shape=jax.ShapeDtypeStruct((ROWS, D), BF), in_...  168 us

profile of v2, /device:TPU:2, one launch (start us, length us, event | category | flops | bytes accessed | tf_op | source)
XLA Modules:
  0.0 172.0 jit_solution(11778019896721856627)
XLA Ops:
  0.0 1.3 select_reduce_fusion.wt_ref
  1.3 168.0 %moe.1 = bf16[128,6144]{1,0:T(8,128)(2,1)} custom-call(f32[16,128]{1,0:T(8,128)} %select_reduce_fusion.wt_ref, bf16[128,6144]{1,0:T(8,128)(2,1)} %tok_ref.1, bf16[1,336,6144]{2,1,0:T(8,128)(2,1)} %wg_ref.1, bf16[1,336,6144]{2,1,0:T(8,128)(2,1)} %wd_ref.1), custom_call_target="tpu_custom_call" | custom-call | flops 16911433728 | bytes 16515072 | tf_op jit(solution)/shard_map/moe/pallas_call | solution.py:505
  169.3 2.7 %copy.7 = bf16[128,6144]{1,0:T(8,128)(2,1)} copy(bf16[128,6144]{1,0:T(8,128)(2,1)} %moe.1) | data formatting | bytes 3145728

commit v3 on v2

--- a/solution.py
+++ b/solution.py
@@ -20,20 +20,22 @@
 CW = HALF // NS
 HW = CW // 2
 NJ = 2 * NS
+EARLY = 3
+CAP = 64
 RSLOT = {0: 0, 1: 1, 3: 2, 2: 3}
 
 
 def kernel(
     wt_ref, tok_ref, wg_ref, wd_ref, o_ref,
-    xp, pb, wg, wd, pre, es, er, hid, wt,
-    ry1, ry2, rx1, rx2, tz, fz,
+    xp, pb, wg, wd, pre, es, er, hid, wt, pick,
+    ry1, ry2, rx, tz, fz,
     tok_sem,
     wgo, wgs, wgr, wgzs, wgzr, wgls, wglr,
     wdo, wds, wdr, wdzs, wdzr, wdls, wdlr,
     wts, wtr,
     s1s, s1r, s2s, s2r, os_, or_, is_, ir_, exs, exr,
-    y1s, y1r, y2s, y2r, x1s, x1r, x2s, x2r,
-    z1s, z1r, ags, agr, aglo,
+    y1s, y1r, y2s, y2r, xs_, xr_,
+    z1s, z1r, ags, agr, aglo, ils, ilr,
 ):
     e = lax.axis_index("expert")
     c = lax.axis_index("cuts")
@@ -49,6 +51,7 @@
     ym = dev(hi, (y + 3) % 4, k, z, lo)
     inner = dev(hi, y, k, z, ol)
     outer = dev(1 - hi, y, k, z, ol)
+    across = dev(1 - hi, y, k, z, lo)
     core = dev(hi, y, 1 - k, z, lo)
 
     def zdev(dz, lo_):
@@ -135,10 +138,10 @@
         for dy in range(4):
             if (dx, dy) != (0, 0):
                 partners.append(rel(dx, dy))
-    for dz in range(8):
-        if dz:
-            partners.append(zdev(dz, lo))
+    for dz in range(1, 8):
+        partners.append(zdev(dz, lo))
         partners.append(zdev(dz, ol))
+    partners += [inner, across]
     for p in partners:
         pl.semaphore_signal(bar, inc=1, device_id=p, device_id_type=MESH)
     loop(NS, start_local)
@@ -185,40 +188,64 @@
             pre[i, row0:row0 + m, :] = acc
 
     def ex(n, d):
-        rows = (pl.ds(0, 384), pl.ds(384, 128), pl.ds(512, 512))[n]
-        return remote(es.at[d, rows], er.at[d, rows], exs.at[n, d], exr.at[n, d], zdev(1 - 2 * d, lo))
+        blocks = pl.ds(4 * n, 4)
+        return remote(es.at[d, blocks], er.at[d, blocks], exs.at[n, d], exr.at[n, d], zdev(1 - 2 * d, lo))
 
     def exchange(n):
-        b0, nb = ((0, 3), (3, 1), (4, 4))[n]
-
-        def stage(b):
-            rows = pl.ds(pl.multiple_of((b0 + b) * ROWS, ROWS), ROWS)
+        def stage(i):
+            b = 4 * n + i
+            rows = pl.ds(pl.multiple_of(b * ROWS, ROWS), ROWS)
             for d in range(2):
-                es[d, rows, :] = pre[d, rows, :].astype(BF)
-
-        loop(nb, stage)
+                for q in range(2):
+                    v = pre[d, rows, q * FFP:(q + 1) * FFP].astype(BF)
+                    es[d, b, :, q * FFP:(q + 1) * FFP] = jnp.dot(
+                        pick[b, q], v, preferred_element_type=F32
+                    ).astype(BF)
+
+        loop(4, stage)
         ex(n, 0).start()
         ex(n, 1).start()
 
-    def first(j):
-        gw.along(j).start()
-        gw.swap(j).start()
-
-    loop(NS, first)
-
-    def l0(j):
+    e0 = 2 * (e // 2)
+
+    def make_pick():
+        got = wt.at[pl.ds(1, 7)]
+        all_wt = remote(got, got, wts, wtr, core)
+        all_wt.wait_send()
+        all_wt.wait_recv()
+        ri = lax.broadcasted_iota(jnp.int32, (ROWS, ROWS), 0)
+        ci = lax.broadcasted_iota(jnp.int32, (ROWS, ROWS), 1)
+        upto = jnp.where(ri <= ci, 1.0, 0.0).astype(BF)
+        row = lax.broadcasted_iota(jnp.int32, (EXPERTS, ROWS), 0)
+        slot = lax.broadcasted_iota(jnp.int32, (CAP, ROWS), 0).astype(F32)
+
+        def block(b):
+            hit = jnp.where(wt[b] > 0.0, 1.0, 0.0)
+            place = jnp.dot(hit.astype(BF), upto, preferred_element_type=F32) * hit - 1.0
+            for q in range(2):
+                mine = jnp.sum(jnp.where(row == e0 + q, place, 0.0), axis=0, keepdims=True)
+                pick[b, q] = jnp.where(slot == mine, 1.0, 0.0).astype(BF)
+
+        loop(8, block)
+
+    def send_own(j):
         load_tok(j, 0).wait()
         load_tok(j, 1).wait()
         s1(j, 0).start()
         s1(j, 1).start()
         og(j, 0).start()
 
-    loop(NS, l0)
+    def swap_gate(j):
+        gw.swap(j).start()
+
+    for j in range(2):
+        gw.along(j).start()
+        send_own(j)
+    loop(NS, swap_gate)
     for dx in range(2):
         for dy in range(4):
             if (dx, dy) != (0, 0):
                 remote(wt_ref, wt.at[dx * 4 + RSLOT[(4 - dy) % 4]], wts, wtr, rel(dx, dy)).start()
-    dw.along(0).start()
 
     def clear_pre(b):
         rows = pl.ds(pl.multiple_of(b * ROWS, ROWS), ROWS)
@@ -227,7 +254,10 @@
 
     loop(8, clear_pre)
 
-    def l1(t):
+    def at(t, lag):
+        return jnp.logical_and(t >= lag, t < NS + lag)
+
+    def g_tick(t):
         @pl.when(t < NS)
         def _():
             s1(t, 0).wait_recv()
@@ -235,60 +265,64 @@
             s1(t, 1).wait_recv()
             s2(t, 1).start()
             og(t, 1).start()
+
+        @pl.when(t + 2 < NS)
+        def _():
+            send_own(t + 2)
+            gw.along(t + 2).start()
+
+        @pl.when(jnp.logical_and(t + 2 >= NS, t + 2 < NS + 4))
+        def _():
+            dw.along(t + 2 - NS).start()
+
+        @pl.when(t < NS)
+        def _():
             og(t, 0).wait_recv()
             ig(t, 0).start()
+            dw.swap(t).start()
+
+        @pl.when(at(t, 1))
+        def _():
+            s2(t - 1, 0).wait_recv()
+            s2(t - 1, 1).wait_recv()
+            og(t - 1, 2).start()
+
+        @pl.when(at(t, 2))
+        def _():
+            og(t - 2, 1).wait_recv()
+            ig(t - 2, 1).start()
+
+        @pl.when(at(t, 3))
+        def _():
+            og(t - 3, 2).wait_recv()
+            ig(t - 3, 2).start()
+
+        @pl.when(t < NS)
+        def _():
             gw.along(t).wait_recv()
             gw.relay(t).start()
 
-        @pl.when(jnp.logical_and(t >= 2, t < NS))
-        def _():
-            og(t - 2, 1).wait_recv()
-            ig(t - 2, 1).start()
-
-        @pl.when(t >= 1)
+        @pl.when(t == 2)
+        def _():
+            make_pick()
+
+        @pl.when(at(t, 1))
         def _():
             gw.ready(t - 1)
-            gate(t - 1, 0, 0, 3)
-
-    loop(NS + 1, l1)
-    exchange(0)
-
-    def l2(j):
-        s2(j, 0).wait_recv()
-        s2(j, 1).wait_recv()
-        og(j, 2).start()
-
-        @pl.when(j < 2)
-        def _():
-            og(j + 4, 1).wait_recv()
-            ig(j + 4, 1).start()
-
-        dw.swap(j).start()
-        gate(j, 0, 3, 1)
-
-    loop(NS, l2)
+            gate(t - 1, 0, 0, 4)
+
+        @pl.when(t == NS)
+        def _():
+            exchange(0)
+
+        @pl.when(at(t, 4))
+        def _():
+            for n in range(3):
+                ig(t - 4, n).wait_recv()
+            gate(t - 4, 1, 0, 4)
+
+    loop(NS + 4, g_tick)
     exchange(1)
-    dw.along(1).start()
-
-    def l3(t):
-        @pl.when(t < NS)
-        def _():
-            og(t, 2).wait_recv()
-            ig(t, 2).start()
-
-        @pl.when(t >= 2)
-        def _():
-            for n in range(3):
-                ig(t - 2, n).wait_recv()
-            gate(t - 2, 1, 0, 4)
-
-    loop(NS + 2, l3)
-    exchange(2)
-
-    def more(s):
-        dw.along(s + 2).start()
-
-    loop(NS - 2, more)
 
     def relay_down(s):
         dw.along(s).wait_recv()
@@ -296,13 +330,8 @@
 
     relay_down(0)
 
-    got = wt.at[pl.ds(1, 7)]
-    all_wt = remote(got, got, wts, wtr, core)
-    all_wt.wait_send()
-    all_wt.wait_recv()
     col = lax.broadcasted_iota(jnp.int32, (EXPERTS, PAIR), 1)
     row = lax.broadcasted_iota(jnp.int32, (EXPERTS, PAIR), 0)
-    e0 = 2 * (e // 2)
     hit0 = jnp.logical_and(row == e0, col < FF)
     hit1 = jnp.logical_and(row == e0 + 1, jnp.logical_and(col >= FFP, col < FFP + FF))
     sel = jnp.where(jnp.logical_or(hit0, hit1), 1.0, 0.0).astype(F32)
@@ -314,12 +343,17 @@
             preferred_element_type=F32, precision=lax.Precision.HIGHEST,
         )
         for i in range(2):
-            v = pre[i, rows, :] + er[1 - i, rows, :].astype(F32)
-            hid[rows, i * PAIR:(i + 1) * PAIR] = (scale * (v / (1.0 + jnp.exp(-v)))).astype(BF)
-
-    for n in range(2):
-        ex(n, 0).wait_recv()
-        ex(n, 1).wait_recv()
+            for q in range(2):
+                at = slice(q * FFP, (q + 1) * FFP)
+                more = lax.dot_general(
+                    pick[b, q], er[1 - i, b, :, at], (((0,), (0,)), ((), ())), preferred_element_type=F32
+                )
+                v = pre[i, rows, at] + more
+                to = i * PAIR + q * FFP
+                hid[rows, to:to + FFP] = (scale[:, at] * (v / (1.0 + jnp.exp(-v)))).astype(BF)
+
+    ex(0, 0).wait_recv()
+    ex(0, 1).wait_recv()
     loop(4, hidden)
     relay_down(1)
 
@@ -337,8 +371,6 @@
             acc = acc + p.astype(F32)
         return acc.astype(BF)
 
-    top, low = pl.ds(0, 64), pl.ds(64, 64)
-
     def a1(s, dx, d):
         return remote(pb.at[s, d, dx, 3], ry1.at[s, dx, d], y1s.at[s, dx, d], y1r.at[s, dx, d], yp if d == 0 else ym)
 
@@ -347,16 +379,9 @@
             pb.at[s, :, dx, 1 + d], ry2.at[s, dx, d], y2s.at[s, dx, d], y2r.at[s, dx, d], yp if d == 0 else ym
         )
 
-    def a3(s, d):
-        return remote(
-            pb.at[s, lo, 1, 0, top if d == 0 else low], rx1.at[s, d],
-            x1s.at[s, d], x1r.at[s, d], inner if d == 0 else outer,
-        )
-
-    def a4(s, d):
-        return remote(
-            pb.at[s, ol, d, 0], rx2.at[s, d], x2s.at[s, d], x2r.at[s, d], inner if d == 0 else outer
-        )
+    def a3(s, n):
+        src = pb.at[s, ol, n, 0] if n < 2 else pb.at[s, lo, 1, 0]
+        return remote(src, rx.at[s, n], xs_.at[s, n], xr_.at[s, n], (inner, outer, across)[n])
 
     def z1(s):
         for dz in range(1, 4):
@@ -379,28 +404,41 @@
 
     def z2(s):
         keep(s).start()
-        for dz in range(8):
-            if dz:
-                remote(fz.at[s], place(s), ags.at[s], agr.at[s], zdev(dz, lo)).start()
-            remote(fz.at[s], place(s), ags.at[s], agr.at[s], zdev(dz, ol)).start()
+        for dz in range(1, 8):
+            remote(fz.at[s], place(s), ags.at[s], agr.at[s], zdev(dz, lo)).start()
+
+        @pl.when(s == NS - 1)
+        def _():
+            for dz in range(8):
+                remote(fz.at[s], place(s), ils.at[s, dz % 2], ilr.at[s, zpar], zdev(dz, ol)).start()
 
     def z2_done(s):
         return remote(tz.at[s], tz.at[s], ags.at[s], agr.at[s], core)
 
+    def cross(s, par):
+        at = pl.multiple_of(par * HALF + s * CW + lo * HW, HW)
+        ref = o_ref.at[:, pl.ds(at, HW)]
+        return remote(ref, ref, ils.at[s, par], ilr.at[s, par], inner)
+
     def job(t):
-        early = t < 4
-        return jnp.where(early, t % 2, t // 2), jnp.where(early, t // 2, t % 2)
+        early = t < 2 * EARLY
+        return jnp.where(early, t % EARLY, t // 2), jnp.where(early, t // EARLY, t % 2)
 
     def r_tick(t):
-        @pl.when(t == 2)
-        def _():
-            ex(2, 0).wait_recv()
-            ex(2, 1).wait_recv()
+        @pl.when(t == EARLY)
+        def _():
+            ex(1, 0).wait_recv()
+            ex(1, 1).wait_recv()
+            dw.along(4).start()
 
             def late(b):
                 hidden(b + 4)
 
             loop(4, late)
+
+        @pl.when(t == EARLY + 1)
+        def _():
+            dw.along(5).start()
 
         @pl.when(t < NJ)
         def _():
@@ -422,34 +460,31 @@
                 pb[s, d, dx, 1 + d] = total(pb[s, d, dx, 1 + d], ry1[s, dx, d])
                 a2(s, dx, d).start()
 
-        @pl.when(jnp.logical_and(t >= 2, t - 2 < NJ))
-        def _():
-            s, dx = job(t - 2)
+        @pl.when(jnp.logical_and(t >= 3, t - 3 < NJ))
+        def _():
+            s, dx = job(t - 3)
             a2(s, dx, 0).wait_recv()
             a2(s, dx, 1).wait_recv()
             pb[s, :, dx, 0] = total(pb[s, :, dx, 0], ry2[s, dx, 0], ry2[s, dx, 1])
 
         def stage(n, fn):
-            @pl.when(jnp.logical_and(t % 2 == n % 2, jnp.logical_and(t >= n, t - n < NJ)))
+            u = t - EARLY - n
+            near = jnp.logical_and(u >= 0, u < EARLY)
+            s = jnp.where(near, u, (u + EARLY - 1) // 2)
+            far = jnp.logical_and((u + EARLY - 1) % 2 == 0, jnp.logical_and(u > EARLY, s < NS))
+
+            @pl.when(jnp.logical_or(near, far))
             def _():
-                fn((t - n) // 2)
-
-        def go_x1(s):
-            a3(s, 0).start()
-            a3(s, 1).start()
-
-        def go_x2(s):
-            a3(s, 0).wait_recv()
-            pb[s, ol, 1, 0, 0:64] = total(pb[s, ol, 1, 0, 0:64], rx1[s, 0])
-            a4(s, 1).start()
-            a3(s, 1).wait_recv()
-            pb[s, ol, 0, 0, 64:128] = total(pb[s, ol, 0, 0, 64:128], rx1[s, 1])
-            a4(s, 0).start()
+                fn(s)
+
+        def go_x(s):
+            for n in range(3):
+                a3(s, n).start()
 
         def go_z1(s):
-            a4(s, 0).wait_recv()
-            a4(s, 1).wait_recv()
-            tz[s, 0:4] = total(pb[s, lo, 0, 0], rx2[s, 0], rx2[s, 1]).reshape(4, 32, HW)
+            for n in range(3):
+                a3(s, n).wait_recv()
+            tz[s, 0:4] = total(pb[s, lo, 0, 0], rx[s, 0], rx[s, 1], rx[s, 2]).reshape(4, 32, HW)
             z1(s)
 
         def go_z2(s):
@@ -457,16 +492,29 @@
             fz[s] = total(tz[s, zi], tz[s, 4], tz[s, 5], tz[s, 6])
             z2(s)
 
-        stage(4, go_x1)
-        stage(5, go_x2)
-        stage(6, go_z1)
+        def go_cross(s):
+            keep(s).wait()
+            z2_done(s).wait_recv()
+
+            @pl.when(s < NS - 1)
+            def _():
+                cross(s, 0).start()
+                cross(s, 1).start()
+
+        stage(3, go_x)
+        stage(5, go_z1)
         stage(7, go_z2)
-
-        @pl.when(jnp.logical_and(t % 2 == 1, jnp.logical_and(t >= 3, t < NJ - 1)))
-        def _():
-            relay_down((t + 1) // 2)
-
-    loop(NJ + 6, r_tick)
+        stage(9, go_cross)
+
+        ahead = t + 2 < EARLY
+        late_s = t // 2 + 1
+        follow = jnp.logical_and(t % 2 == 0, jnp.logical_and(late_s >= EARLY, late_s < NS))
+
+        @pl.when(jnp.logical_or(ahead, follow))
+        def _():
+            relay_down(jnp.where(ahead, t + 2, late_s))
+
+    loop(NJ + 9, r_tick)
 
     def drain(s):
         gw.drain(s)
@@ -474,21 +522,21 @@
         for d in range(2):
             s1(s, d).wait_send()
             s2(s, d).wait_send()
-            a3(s, d).wait_send()
-            a4(s, d).wait_send()
             for dx in range(2):
                 a1(s, dx, d).wait_send()
                 a2(s, dx, d).wait_send()
         for n in range(3):
+            a3(s, n).wait_send()
             og(s, n).wait_send()
             ig(s, n).wait_send()
         z1_done(s).wait_send()
-        keep(s).wait()
         z2_done(s).wait_send()
-        z2_done(s).wait_recv()
+        for par in range(2):
+            cross(s, par).wait_send()
+            cross(s, par).wait_recv()
 
     loop(NS, drain)
-    for n in range(3):
+    for n in range(2):
         ex(n, 0).wait_send()
         ex(n, 1).wait_send()
 
@@ -499,8 +547,8 @@
     dma = pltpu.SemaphoreType.DMA
     sems = (
         [dma((NS, 2))] + [dma((NS,))] * 14 + [dma, dma]
-        + [dma((NS, 2))] * 4 + [dma((NS, 3))] * 4 + [dma((3, 2))] * 2
-        + [dma((NS, 2, 2))] * 4 + [dma((NS, 2))] * 4 + [dma((NS,))] * 5
+        + [dma((NS, 2))] * 4 + [dma((NS, 3))] * 4 + [dma((2, 2))] * 2
+        + [dma((NS, 2, 2))] * 4 + [dma((NS, 3))] * 2 + [dma((NS,))] * 5 + [dma((NS, 2))] * 2
     )
     return pl.pallas_call(
         kernel,
@@ -513,15 +561,15 @@
             pltpu.VMEM((NS, 4, FFP, CW), BF),
             pltpu.VMEM((NS, 4, FFP, CW), BF),
             pltpu.VMEM((2, 8 * ROWS, PAIR), F32),
-            pltpu.VMEM((2, 8 * ROWS, PAIR), BF),
-            pltpu.VMEM((2, 8 * ROWS, PAIR), BF),
+            pltpu.VMEM((2, 8, CAP, PAIR), BF),
+            pltpu.VMEM((2, 8, CAP, PAIR), BF),
             pltpu.VMEM((8 * ROWS, 2 * PAIR), BF),
             pltpu.VMEM((8, EXPERTS, ROWS), F32),
+            pltpu.VMEM((8, 2, CAP, ROWS), BF),
             pltpu.VMEM((NS, 2, 2, ROWS, HW), BF),
             pltpu.VMEM((NS, 2, 2, 2, ROWS, HW), BF),
-            pltpu.VMEM((NS, 2, 64, HW), BF),
-            pltpu.VMEM((NS, 2, ROWS, HW), BF),
-            pltpu.VMEM((NS, 15, 32, HW), BF),
+            pltpu.VMEM((NS, 3, ROWS, HW), BF),
+            pltpu.VMEM((NS, 7, 32, HW), BF),
             pltpu.VMEM((NS, 32, HW), BF),
         ] + sems,
         compiler_params=pltpu.CompilerParams(

time: 173 us -> 146 us (0.84)
  Pallas kernels: 168 us -> 142 us
    pallas_call x1, Pallas kernels: 168 us -> 142 us  [on_device(): pl.pallas_call(kernel, out_shape=jax.ShapeDtypeStruct((ROWS, D), BF), in_...]
where the time goes in v3:
time: 146 us
  Pallas kernels  142 us (97%)
  local copies, waits for them, and re-layouts  2.69 us (2%)
    pallas_call x1, Pallas kernels, on_device(): pl.pallas_call(kernel, out_shape=jax.ShapeDtypeStruct((ROWS, D), BF), in_...  142 us

profile of v3, /device:TPU:2, one launch (start us, length us, event | category | flops | bytes accessed | tf_op | source)
XLA Modules:
  0.0 146.2 jit_solution(920681542305311006)
XLA Ops:
  0.0 1.3 select_reduce_fusion.wt_ref
  1.3 142.2 %moe.1 = bf16[128,6144]{1,0:T(8,128)(2,1)} custom-call(f32[16,128]{1,0:T(8,128)} %select_reduce_fusion.wt_ref, bf16[128,6144]{1,0:T(8,128)(2,1)} %tok_ref.1, bf16[1,336,6144]{2,1,0:T(8,128)(2,1)} %wg_ref.1, bf16[1,336,6144]{2,1,0:T(8,128)(2,1)} %wd_ref.1), custom_call_target="tpu_custom_call" | custom-call | flops 16911433728 | bytes 16515072 | tf_op jit(solution)/shard_map/moe/pallas_call | solution.py:553
  143.5 2.7 %copy.7 = bf16[128,6144]{1,0:T(8,128)(2,1)} copy(bf16[128,6144]{1,0:T(8,128)(2,1)} %moe.1) | data formatting | bytes 3145728

commit v4 on v3

--- a/solution.py
+++ b/solution.py
@@ -19,8 +19,15 @@
 NS = 6
 CW = HALF // NS
 HW = CW // 2
-NJ = 2 * NS
+NX = 1
+XFIRST = 3
+NY = NS - NX
+NJ = 2 * NY
 EARLY = 3
+LAGS = (3, 5, 7, 9)
+XTICKS = ((4, 8, 9, 11, 13, 15),)
+NT = 19
+LATE = 5
 CAP = 64
 RSLOT = {0: 0, 1: 1, 3: 2, 2: 3}
 
@@ -28,13 +35,14 @@
 def kernel(
     wt_ref, tok_ref, wg_ref, wd_ref, o_ref,
     xp, pb, wg, wd, pre, es, er, hid, wt, pick,
-    ry1, ry2, rx, tz, fz,
+    ry1, ry2, rx, qx, qy1, qy2, tz, fz,
     tok_sem,
     wgo, wgs, wgr, wgzs, wgzr, wgls, wglr,
     wdo, wds, wdr, wdzs, wdzr, wdls, wdlr,
     wts, wtr,
     s1s, s1r, s2s, s2r, os_, or_, is_, ir_, exs, exr,
     y1s, y1r, y2s, y2r, xs_, xr_,
+    b1s, b1r, b2s, b2r, b3s, b3r,
     z1s, z1r, ags, agr, aglo, ils, ilr,
 ):
     e = lax.axis_index("expert")
@@ -271,9 +279,9 @@
             send_own(t + 2)
             gw.along(t + 2).start()
 
-        @pl.when(jnp.logical_and(t + 2 >= NS, t + 2 < NS + 4))
-        def _():
-            dw.along(t + 2 - NS).start()
+        @pl.when(jnp.logical_and(t >= 3, t < 6))
+        def _():
+            dw.along(t - 3).start()
 
         @pl.when(t < NS)
         def _():
@@ -371,17 +379,39 @@
             acc = acc + p.astype(F32)
         return acc.astype(BF)
 
-    def a1(s, dx, d):
-        return remote(pb.at[s, d, dx, 3], ry1.at[s, dx, d], y1s.at[s, dx, d], y1r.at[s, dx, d], yp if d == 0 else ym)
-
-    def a2(s, dx, d):
+    def ychunk(i):
+        return jnp.where(i < XFIRST, i, i + NX)
+
+    def yto(d):
+        return yp if d == 0 else ym
+
+    def a1(i, dx, d):
+        return remote(pb.at[ychunk(i), d, dx, 3], ry1.at[i, dx, d], y1s.at[i, dx, d], y1r.at[i, dx, d], yto(d))
+
+    def a2(i, dx, d):
         return remote(
-            pb.at[s, :, dx, 1 + d], ry2.at[s, dx, d], y2s.at[s, dx, d], y2r.at[s, dx, d], yp if d == 0 else ym
+            pb.at[ychunk(i), :, dx, 1 + d], ry2.at[i, dx, d], y2s.at[i, dx, d], y2r.at[i, dx, d], yto(d)
         )
 
-    def a3(s, n):
+    def a3(i, n):
+        s = ychunk(i)
         src = pb.at[s, ol, n, 0] if n < 2 else pb.at[s, lo, 1, 0]
-        return remote(src, rx.at[s, n], xs_.at[s, n], xr_.at[s, n], (inner, outer, across)[n])
+        return remote(src, rx.at[i, n], xs_.at[i, n], xr_.at[i, n], (inner, outer, across)[n])
+
+    half = (pl.ds(0, 64), pl.ds(64, 64))
+
+    def b1(i, n):
+        s = XFIRST + i
+        src = pb.at[s, ol, n] if n < 2 else pb.at[s, lo, 1]
+        return remote(src, qx.at[i, n], b1s.at[i, n], b1r.at[i, n], (inner, outer, across)[n])
+
+    def b2(i, d):
+        return remote(
+            pb.at[XFIRST + i, lo, 0, 3, half[d]], qy1.at[i, d], b2s.at[i, d], b2r.at[i, d], yto(d)
+        )
+
+    def b3(i, d):
+        return remote(pb.at[XFIRST + i, lo, 0, 1 + d], qy2.at[i, d], b3s.at[i, d], b3r.at[i, d], yto(d))
 
     def z1(s):
         for dz in range(1, 4):
@@ -393,33 +423,42 @@
         ref = tz.at[s, pl.ds(4, 3)]
         return remote(ref, ref, z1s.at[s], z1r.at[s], core)
 
-    def place(s):
+    def place(s, lo_):
         return o_ref.at[
             pl.ds(pl.multiple_of(zi * 32, 32), 32),
-            pl.ds(pl.multiple_of(zpar * HALF + s * CW + lo * HW, HW), HW),
+            pl.ds(pl.multiple_of(zpar * HALF + s * CW + lo_ * HW, HW), HW),
         ]
 
     def keep(s):
-        return pltpu.make_async_copy(fz.at[s], place(s), aglo.at[s])
+        return pltpu.make_async_copy(fz.at[s], place(s, lo), aglo.at[s])
 
     def z2(s):
         keep(s).start()
         for dz in range(1, 8):
-            remote(fz.at[s], place(s), ags.at[s], agr.at[s], zdev(dz, lo)).start()
-
-        @pl.when(s == NS - 1)
+            remote(fz.at[s], place(s, lo), ags.at[s], agr.at[s], zdev(dz, lo)).start()
+
+        @pl.when(s >= LATE)
         def _():
             for dz in range(8):
-                remote(fz.at[s], place(s), ils.at[s, dz % 2], ilr.at[s, zpar], zdev(dz, ol)).start()
-
-    def z2_done(s):
-        return remote(tz.at[s], tz.at[s], ags.at[s], agr.at[s], core)
+                remote(fz.at[s], place(s, lo), ils.at[s, dz % 2], ilr.at[s, zpar], zdev(dz, ol)).start()
 
     def cross(s, par):
         at = pl.multiple_of(par * HALF + s * CW + lo * HW, HW)
         ref = o_ref.at[:, pl.ds(at, HW)]
         return remote(ref, ref, ils.at[s, par], ilr.at[s, par], inner)
 
+    def z3(s):
+        keep(s).wait()
+        z2_done(s).wait_recv()
+
+        @pl.when(s < LATE)
+        def _():
+            cross(s, 0).start()
+            cross(s, 1).start()
+
+    def z2_done(s):
+        return remote(tz.at[s], tz.at[s], ags.at[s], agr.at[s], core)
+
     def job(t):
         early = t < 2 * EARLY
         return jnp.where(early, t % EARLY, t // 2), jnp.where(early, t // EARLY, t % 2)
@@ -429,92 +468,137 @@
         def _():
             ex(1, 0).wait_recv()
             ex(1, 1).wait_recv()
+            dw.along(3).start()
             dw.along(4).start()
+            dw.along(5).start()
 
             def late(b):
                 hidden(b + 4)
 
             loop(4, late)
 
-        @pl.when(t == EARLY + 1)
-        def _():
-            dw.along(5).start()
-
         @pl.when(t < NJ)
         def _():
-            s, dx = job(t)
+            i, dx = job(t)
+            s = ychunk(i)
 
             @pl.when(dx == 0)
             def _():
                 dw.ready(s)
 
             down(s, dx)
-            a1(s, dx, 0).start()
-            a1(s, dx, 1).start()
+            a1(i, dx, 0).start()
+            a1(i, dx, 1).start()
 
         @pl.when(jnp.logical_and(t >= 1, t - 1 < NJ))
         def _():
-            s, dx = job(t - 1)
+            i, dx = job(t - 1)
+            s = ychunk(i)
             for d in range(2):
-                a1(s, dx, d).wait_recv()
-                pb[s, d, dx, 1 + d] = total(pb[s, d, dx, 1 + d], ry1[s, dx, d])
-                a2(s, dx, d).start()
-
-        @pl.when(jnp.logical_and(t >= 3, t - 3 < NJ))
-        def _():
-            s, dx = job(t - 3)
-            a2(s, dx, 0).wait_recv()
-            a2(s, dx, 1).wait_recv()
-            pb[s, :, dx, 0] = total(pb[s, :, dx, 0], ry2[s, dx, 0], ry2[s, dx, 1])
+                a1(i, dx, d).wait_recv()
+                pb[s, d, dx, 1 + d] = total(pb[s, d, dx, 1 + d], ry1[i, dx, d])
+                a2(i, dx, d).start()
+
+        @pl.when(jnp.logical_and(t >= LAGS[0], t - LAGS[0] < NJ))
+        def _():
+            i, dx = job(t - LAGS[0])
+            s = ychunk(i)
+            a2(i, dx, 0).wait_recv()
+            a2(i, dx, 1).wait_recv()
+            pb[s, :, dx, 0] = total(pb[s, :, dx, 0], ry2[i, dx, 0], ry2[i, dx, 1])
 
         def stage(n, fn):
             u = t - EARLY - n
             near = jnp.logical_and(u >= 0, u < EARLY)
-            s = jnp.where(near, u, (u + EARLY - 1) // 2)
-            far = jnp.logical_and((u + EARLY - 1) % 2 == 0, jnp.logical_and(u > EARLY, s < NS))
+            i = jnp.where(near, u, (u + EARLY - 1) // 2)
+            far = jnp.logical_and((u + EARLY - 1) % 2 == 0, jnp.logical_and(u > EARLY, i < NY))
 
             @pl.when(jnp.logical_or(near, far))
             def _():
-                fn(s)
-
-        def go_x(s):
+                fn(i)
+
+        def go_x(i):
             for n in range(3):
-                a3(s, n).start()
-
-        def go_z1(s):
+                a3(i, n).start()
+
+        def go_z1(i):
+            s = ychunk(i)
             for n in range(3):
-                a3(s, n).wait_recv()
-            tz[s, 0:4] = total(pb[s, lo, 0, 0], rx[s, 0], rx[s, 1], rx[s, 2]).reshape(4, 32, HW)
+                a3(i, n).wait_recv()
+            tz[s, 0:4] = total(pb[s, lo, 0, 0], rx[i, 0], rx[i, 1], rx[i, 2]).reshape(4, 32, HW)
             z1(s)
 
-        def go_z2(s):
+        def sum_z(s):
             z1_done(s).wait_recv()
             fz[s] = total(tz[s, zi], tz[s, 4], tz[s, 5], tz[s, 6])
             z2(s)
 
-        def go_cross(s):
-            keep(s).wait()
-            z2_done(s).wait_recv()
-
-            @pl.when(s < NS - 1)
-            def _():
-                cross(s, 0).start()
-                cross(s, 1).start()
-
-        stage(3, go_x)
-        stage(5, go_z1)
-        stage(7, go_z2)
-        stage(9, go_cross)
-
-        ahead = t + 2 < EARLY
-        late_s = t // 2 + 1
-        follow = jnp.logical_and(t % 2 == 0, jnp.logical_and(late_s >= EARLY, late_s < NS))
-
-        @pl.when(jnp.logical_or(ahead, follow))
-        def _():
-            relay_down(jnp.where(ahead, t + 2, late_s))
-
-    loop(NJ + 9, r_tick)
+        def go_z2(i):
+            sum_z(ychunk(i))
+
+        def go_z3(i):
+            z3(ychunk(i))
+
+        def x_first(i):
+            s = XFIRST + i
+            dw.ready(s)
+            down(s, 1)
+            b1(i, 1).start()
+            b1(i, 2).start()
+            down(s, 0)
+            b1(i, 0).start()
+
+        def x_sum(i):
+            s = XFIRST + i
+            for n in range(3):
+                b1(i, n).wait_recv()
+            for r in (3, 1, 2, 0):
+                pb[s, lo, 0, r] = total(pb[s, lo, 0, r], qx[i, 0, r], qx[i, 1, r], qx[i, 2, r])
+                if r == 3:
+                    b2(i, 0).start()
+                    b2(i, 1).start()
+
+        def x_y2(i):
+            s = XFIRST + i
+            for d in range(2):
+                b2(i, d).wait_recv()
+                rows = slice(64 * d, 64 * d + 64)
+                pb[s, lo, 0, 1 + d, rows] = total(pb[s, lo, 0, 1 + d, rows], qy1[i, d])
+                b3(i, d).start()
+
+        def x_z1(i):
+            s = XFIRST + i
+            b3(i, 0).wait_recv()
+            b3(i, 1).wait_recv()
+            tz[s, 0:4] = total(pb[s, lo, 0, 0], qy2[i, 0], qy2[i, 1]).reshape(4, 32, HW)
+            z1(s)
+
+        def x_z2(i):
+            sum_z(XFIRST + i)
+
+        def x_z3(i):
+            z3(XFIRST + i)
+
+        steps = (x_first, x_sum, x_y2, x_z1, x_z2, x_z3)
+        stage(LAGS[0], go_x)
+        stage(LAGS[1], go_z1)
+        stage(LAGS[2], go_z2)
+        stage(LAGS[3], go_z3)
+        for i in range(NX):
+            for fn, when in zip(steps, XTICKS[i]):
+                @pl.when(t == when)
+                def _(fn=fn, i=i):
+                    fn(i)
+
+        @pl.when(t == 0)
+        def _():
+            relay_down(2)
+
+        @pl.when(jnp.logical_and(t >= 3, t < 6))
+        def _():
+            relay_down(t)
+
+    loop(NT, r_tick)
 
     def drain(s):
         gw.drain(s)
@@ -522,11 +606,7 @@
         for d in range(2):
             s1(s, d).wait_send()
             s2(s, d).wait_send()
-            for dx in range(2):
-                a1(s, dx, d).wait_send()
-                a2(s, dx, d).wait_send()
         for n in range(3):
-            a3(s, n).wait_send()
             og(s, n).wait_send()
             ig(s, n).wait_send()
         z1_done(s).wait_send()
@@ -536,6 +616,24 @@
             cross(s, par).wait_recv()
 
     loop(NS, drain)
+
+    def drain_y(i):
+        for n in range(3):
+            a3(i, n).wait_send()
+        for dx in range(2):
+            for d in range(2):
+                a1(i, dx, d).wait_send()
+                a2(i, dx, d).wait_send()
+
+    def drain_x(i):
+        for n in range(3):
+            b1(i, n).wait_send()
+        for d in range(2):
+            b2(i, d).wait_send()
+            b3(i, d).wait_send()
+
+    loop(NY, drain_y)
+    loop(NX, drain_x)
     for n in range(2):
         ex(n, 0).wait_send()
         ex(n, 1).wait_send()
@@ -548,7 +646,9 @@
     sems = (
         [dma((NS, 2))] + [dma((NS,))] * 14 + [dma, dma]
         + [dma((NS, 2))] * 4 + [dma((NS, 3))] * 4 + [dma((2, 2))] * 2
-        + [dma((NS, 2, 2))] * 4 + [dma((NS, 3))] * 2 + [dma((NS,))] * 5 + [dma((NS, 2))] * 2
+        + [dma((NY, 2, 2))] * 4 + [dma((NY, 3))] * 2
+        + [dma((NX, 3))] * 2 + [dma((NX, 2))] * 4
+        + [dma((NS,))] * 5 + [dma((NS, 2))] * 2
     )
     return pl.pallas_call(
         kernel,
@@ -566,9 +666,12 @@
             pltpu.VMEM((8 * ROWS, 2 * PAIR), BF),
             pltpu.VMEM((8, EXPERTS, ROWS), F32),
             pltpu.VMEM((8, 2, CAP, ROWS), BF),
-            pltpu.VMEM((NS, 2, 2, ROWS, HW), BF),
-            pltpu.VMEM((NS, 2, 2, 2, ROWS, HW), BF),
-            pltpu.VMEM((NS, 3, ROWS, HW), BF),
+            pltpu.VMEM((NY, 2, 2, ROWS, HW), BF),
+            pltpu.VMEM((NY, 2, 2, 2, ROWS, HW), BF),
+            pltpu.VMEM((NY, 3, ROWS, HW), BF),
+            pltpu.VMEM((NX, 3, 4, ROWS, HW), BF),
+            pltpu.VMEM((NX, 2, ROWS // 2, HW), BF),
+            pltpu.VMEM((NX, 2, ROWS, HW), BF),
             pltpu.VMEM((NS, 7, 32, HW), BF),
             pltpu.VMEM((NS, 32, HW), BF),
         ] + sems,

time: 146 us -> 140 us (0.959)
  Pallas kernels: 142 us -> 136 us
    pallas_call x1, Pallas kernels: 142 us -> 136 us  [on_device(): pl.pallas_call(kernel, out_shape=jax.ShapeDtypeStruct((ROWS, D), BF), in_...]
where the time goes in v4:
time: 140 us
  Pallas kernels  136 us (97%)
  local copies, waits for them, and re-layouts  2.69 us (2%)
    pallas_call x1, Pallas kernels, on_device(): pl.pallas_call(kernel, out_shape=jax.ShapeDtypeStruct((ROWS, D), BF), in_...  136 us

profile of v4, /device:TPU:2, one launch (start us, length us, event | category | flops | bytes accessed | tf_op | source)
XLA Modules:
  0.0 139.9 jit_solution(182889415080205182)
XLA Ops:
  0.0 1.3 select_reduce_fusion.wt_ref
  1.3 135.9 %moe.1 = bf16[128,6144]{1,0:T(8,128)(2,1)} custom-call(f32[16,128]{1,0:T(8,128)} %select_reduce_fusion.wt_ref, bf16[128,6144]{1,0:T(8,128)(2,1)} %tok_ref.1, bf16[1,336,6144]{2,1,0:T(8,128)(2,1)} %wg_ref.1, bf16[1,336,6144]{2,1,0:T(8,128)(2,1)} %wd_ref.1), custom_call_target="tpu_custom_call" | custom-call | flops 16911433728 | bytes 16515072 | tf_op jit(solution)/shard_map/moe/pallas_call | solution.py:653
  137.2 2.7 %copy.7 = bf16[128,6144]{1,0:T(8,128)(2,1)} copy(bf16[128,6144]{1,0:T(8,128)(2,1)} %moe.1) | data formatting | bytes 3145728

commit v5 on v4

--- a/solution.py
+++ b/solution.py
@@ -19,6 +19,7 @@
 NS = 6
 CW = HALF // NS
 HW = CW // 2
+LAST = NS - 1
 NX = 1
 XFIRST = 3
 NY = NS - NX
@@ -40,7 +41,7 @@
     wgo, wgs, wgr, wgzs, wgzr, wgls, wglr,
     wdo, wds, wdr, wdzs, wdzr, wdls, wdlr,
     wts, wtr,
-    s1s, s1r, s2s, s2r, os_, or_, is_, ir_, exs, exr,
+    s1s, s1r, s2s, s2r, p1s, p1r, p2s, p2r, os_, or_, is_, ir_, exs, exr,
     y1s, y1r, y2s, y2r, xs_, xr_,
     b1s, b1r, b2s, b2r, b3s, b3r,
     z1s, z1r, ags, agr, aglo, ils, ilr,
@@ -173,6 +174,16 @@
             xp.at[j, d, 0, 2 - d], xp.at[j, d, 0, 3], s2s.at[j, d], s2r.at[j, d], yp if d == 0 else ym
         )
 
+    def p1(d):
+        return remote(
+            xp.at[LAST, :, 1, 0], xp.at[LAST, :, 1, 2 - d], p1s.at[d], p1r.at[d], yp if d == 0 else ym
+        )
+
+    def p2(d):
+        return remote(
+            xp.at[LAST, d, 1, 2 - d], xp.at[LAST, d, 1, 3], p2s.at[d], p2r.at[d], yp if d == 0 else ym
+        )
+
     part = (pl.ds(0, 1), pl.ds(1, 2), pl.ds(3, 1))
 
     def og(j, n):
@@ -236,19 +247,23 @@
 
         loop(8, block)
 
-    def send_own(j):
+    def send_out(j):
         load_tok(j, 0).wait()
         load_tok(j, 1).wait()
+        og(j, 0).start()
+
+    def send_own(j):
         s1(j, 0).start()
         s1(j, 1).start()
-        og(j, 0).start()
 
     def swap_gate(j):
         gw.swap(j).start()
 
     for j in range(2):
         gw.along(j).start()
+        send_out(j)
         send_own(j)
+    send_out(LAST)
     loop(NS, swap_gate)
     for dx in range(2):
         for dy in range(4):
@@ -262,8 +277,8 @@
 
     loop(8, clear_pre)
 
-    def at(t, lag):
-        return jnp.logical_and(t >= lag, t < NS + lag)
+    def at(t, lag, n=NS):
+        return jnp.logical_and(t >= lag, t < n + lag)
 
     def g_tick(t):
         @pl.when(t < NS)
@@ -272,7 +287,14 @@
             s2(t, 0).start()
             s1(t, 1).wait_recv()
             s2(t, 1).start()
+
+        @pl.when(t < LAST)
+        def _():
             og(t, 1).start()
+
+        @pl.when(t + 2 < LAST)
+        def _():
+            send_out(t + 2)
 
         @pl.when(t + 2 < NS)
         def _():
@@ -283,24 +305,47 @@
         def _():
             dw.along(t - 3).start()
 
-        @pl.when(t < NS)
+        @pl.when(t < LAST)
         def _():
             og(t, 0).wait_recv()
             ig(t, 0).start()
+
+        @pl.when(t < NS)
+        def _():
             dw.swap(t).start()
+
+        @pl.when(t == 2)
+        def _():
+            og(LAST, 0).wait_recv()
+            ig(LAST, 0).start()
+
+        @pl.when(t == 4)
+        def _():
+            ig(LAST, 0).wait_recv()
+            p1(0).start()
+            p1(1).start()
+
+        @pl.when(t == 5)
+        def _():
+            for d in range(2):
+                p1(d).wait_recv()
+                p2(d).start()
 
         @pl.when(at(t, 1))
         def _():
             s2(t - 1, 0).wait_recv()
             s2(t - 1, 1).wait_recv()
+
+        @pl.when(at(t, 1, LAST))
+        def _():
             og(t - 1, 2).start()
 
-        @pl.when(at(t, 2))
+        @pl.when(at(t, 2, LAST))
         def _():
             og(t - 2, 1).wait_recv()
             ig(t - 2, 1).start()
 
-        @pl.when(at(t, 3))
+        @pl.when(at(t, 3, LAST))
         def _():
             og(t - 3, 2).wait_recv()
             ig(t - 3, 2).start()
@@ -323,13 +368,19 @@
         def _():
             exchange(0)
 
-        @pl.when(at(t, 4))
+        @pl.when(t == 7)
+        def _():
+            p2(0).wait_recv()
+            p2(1).wait_recv()
+            gate(LAST, 1, 0, 4)
+
+        @pl.when(at(t, 4, LAST))
         def _():
             for n in range(3):
                 ig(t - 4, n).wait_recv()
             gate(t - 4, 1, 0, 4)
 
-    loop(NS + 4, g_tick)
+    loop(LAST + 4, g_tick)
     exchange(1)
 
     def relay_down(s):
@@ -606,9 +657,15 @@
         for d in range(2):
             s1(s, d).wait_send()
             s2(s, d).wait_send()
-        for n in range(3):
-            og(s, n).wait_send()
-            ig(s, n).wait_send()
+        og(s, 0).wait_send()
+        ig(s, 0).wait_send()
+
+        @pl.when(s < LAST)
+        def _():
+            for n in range(1, 3):
+                og(s, n).wait_send()
+                ig(s, n).wait_send()
+
         z1_done(s).wait_send()
         z2_done(s).wait_send()
         for par in range(2):
@@ -634,6 +691,9 @@
 
     loop(NY, drain_y)
     loop(NX, drain_x)
+    for d in range(2):
+        p1(d).wait_send()
+        p2(d).wait_send()
     for n in range(2):
         ex(n, 0).wait_send()
         ex(n, 1).wait_send()
@@ -645,7 +705,7 @@
     dma = pltpu.SemaphoreType.DMA
     sems = (
         [dma((NS, 2))] + [dma((NS,))] * 14 + [dma, dma]
-        + [dma((NS, 2))] * 4 + [dma((NS, 3))] * 4 + [dma((2, 2))] * 2
+        + [dma((NS, 2))] * 4 + [dma((2,))] * 4 + [dma((NS, 3))] * 4 + [dma((2, 2))] * 2
         + [dma((NY, 2, 2))] * 4 + [dma((NY, 3))] * 2
         + [dma((NX, 3))] * 2 + [dma((NX, 2))] * 4
         + [dma((NS,))] * 5 + [dma((NS, 2))] * 2

time: 140 us -> 137 us (0.979)
  Pallas kernels: 136 us -> 133 us
    pallas_call x1, Pallas kernels: 136 us -> 133 us  [on_device(): pl.pallas_call(kernel, out_shape=jax.ShapeDtypeStruct((ROWS, D), BF), in_...]
where the time goes in v5:
time: 137 us
  Pallas kernels  133 us (97%)
  local copies, waits for them, and re-layouts  2.69 us (2%)
    pallas_call x1, Pallas kernels, on_device(): pl.pallas_call(kernel, out_shape=jax.ShapeDtypeStruct((ROWS, D), BF), in_...  133 us

profile of v5, /device:TPU:2, one launch (start us, length us, event | category | flops | bytes accessed | tf_op | source)
XLA Modules:
  0.0 137.0 jit_solution(17755295508608955193)
XLA Ops:
  0.0 1.3 select_reduce_fusion.wt_ref
  1.3 133.0 %moe.1 = bf16[128,6144]{1,0:T(8,128)(2,1)} custom-call(f32[16,128]{1,0:T(8,128)} %select_reduce_fusion.wt_ref, bf16[128,6144]{1,0:T(8,128)(2,1)} %tok_ref.1, bf16[1,336,6144]{2,1,0:T(8,128)(2,1)} %wg_ref.1, bf16[1,336,6144]{2,1,0:T(8,128)(2,1)} %wd_ref.1), custom_call_target="tpu_custom_call" | custom-call | flops 16911433728 | bytes 16515072 | tf_op jit(solution)/shard_map/moe/pallas_call | solution.py:713
  134.3 2.7 %copy.7 = bf16[128,6144]{1,0:T(8,128)(2,1)} copy(bf16[128,6144]{1,0:T(8,128)(2,1)} %moe.1) | data formatting | bytes 3145728
